TPU v7x, 512 devices: a whole 4x8x8 slice. The times are simulated.
512 devices in a mesh: users: 128 (over z, y, core), heads: 4 (over x).
Axes of the slice: x: 4, y: 8, z: 8, core: 2. Of those that a mesh axis runs over, the one named last changes fastest.
Arguments:
- events: bfloat16 [32768, 1024], P('users', 'heads'), may hold values from -6 to 6
- event_owner: int32 [32768, 1], P('users'), may hold values from 0 to 127; in each aligned block of 256 rows (0 to 255, 256 to 511, ...) at most 4 rows name the same one
- event_user: int32 [32768], P('users'), may hold values from 0 to 1
- cache_keys: bfloat16 [128, 2, 512, 1024], P('users', None, None, 'heads'), may hold values from -250 to 250
- cache_values: bfloat16 [128, 2, 512, 1024], P('users', None, None, 'heads'), may hold values from -6 to 6
- cache_len: int32 [128, 2], P('users'), may hold values from 256 to 512
- user_rank: int32 [128, 2], P('users'), may hold values from 0 to 127
- norm_gain: float32 [1024], replicated, may hold values from 0.5 to 1.5
- w_query: bfloat16 [1024, 1024], P(None, 'heads'), may hold values from -0.1875 to 0.1875
- w_key: bfloat16 [1024, 1024], P(None, 'heads'), may hold values from -0.1875 to 0.1875
- w_value: bfloat16 [1024, 1024], P(None, 'heads'), may hold values from -0.1875 to 0.1875
- w_out: bfloat16 [1024, 1024], P('heads'), may hold values from -0.1875 to 0.1875
Outputs:
- refreshed: bfloat16 [128, 512, 1024], P('users', None, 'heads')
- ranked: bfloat16 [128, 256, 1024], P('users', None, 'heads')
Inputs may be any that keep to these rules, and one draw needn't show every extreme that they name: `event_owner`: in the rows of one index of users, no owner is named more than 4 times, a bound that some block reaches.
All inputs are finite; a program needn't handle non-finite values.
Results may differ from a plain program's by a relative error of at most 0.012.
Values may be sent and summed in bfloat16 or wider, within the bound.
No kernel may reach another device: no remote copies, remote signals or barrier semaphores. Data moves between devices by JAX's collectives and lax.ppermute only.
A program may use at most 64 MiB of HBM per device.

v0:
```python
import jax
import jax.numpy as jnp
from jax import lax
from jax.sharding import PartitionSpec as P

HEAD_DIM = 64


def attend(query, keys, values, allowed, head_dim):
    rows = query.shape[0]
    count = keys.shape[0]
    nheads = query.shape[1] // head_dim
    qheads = query.reshape(rows, nheads, head_dim).transpose(1, 0, 2)
    kheads = keys.reshape(count, nheads, head_dim).transpose(1, 0, 2)
    vheads = values.reshape(count, nheads, head_dim).transpose(1, 0, 2)

    def single(pieces):
        qpart, kpart, vpart = pieces
        scores = jnp.dot(qpart, kpart.T, preferred_element_type=jnp.float32) * head_dim ** (-0.5)
        scores = jnp.where(allowed, scores, -jnp.inf)
        top = jnp.max(scores, axis=1, keepdims=True)
        weights = jnp.exp(scores - top)
        probs = (weights / jnp.sum(weights, axis=1, keepdims=True)).astype(jnp.bfloat16)
        return jnp.dot(probs, vpart, preferred_element_type=jnp.float32).astype(jnp.bfloat16)

    outcome = lax.map(single, (qheads, kheads, vheads))
    return outcome.transpose(1, 0, 2).reshape(rows, nheads * head_dim)


def local(
    events,
    event_owner,
    event_user,
    cache_keys,
    cache_values,
    cache_len,
    user_rank,
    norm_gain,
    w_query,
    w_key,
    w_value,
    w_out,
):
    ev_rows, group_width = events.shape
    owners = lax.axis_size("users")
    capacity = max(2, 2 * ev_rows // owners)
    slots = owners * capacity
    owner = event_owner[:, 0]
    onehot = (owner[:, None] == jnp.arange(owners, dtype=jnp.int32)[None, :]).astype(jnp.int32)
    before = jnp.sum(jnp.cumsum(onehot, axis=0) * onehot, axis=1) - 1
    target = owner * capacity + before
    send_rows = jnp.zeros((slots, group_width), jnp.bfloat16).at[target].set(events)
    send_user = jnp.full((slots,), -1, jnp.int32).at[target].set(event_user)
    got_rows, slot_user = (
        lax.all_to_all(send_rows, "users", split_axis=0, concat_axis=0, tiled=True),
        lax.all_to_all(send_user, "users", split_axis=0, concat_axis=0, tiled=True),
    )
    valid = slot_user >= 0
    users = jnp.maximum(slot_user, 0)
    full_rows = lax.all_gather(got_rows, "heads", axis=1, tiled=True)
    wide = full_rows.astype(jnp.float32)
    normed = (
        wide * lax.rsqrt(jnp.mean(wide * wide, axis=1, keepdims=True) + 1e-05) * norm_gain
    ).astype(jnp.bfloat16)
    query = jnp.dot(normed, w_query, preferred_element_type=jnp.float32).astype(jnp.bfloat16)
    key_new = jnp.dot(normed, w_key, preferred_element_type=jnp.float32).astype(jnp.bfloat16)
    value_new = jnp.dot(normed, w_value, preferred_element_type=jnp.float32).astype(jnp.bfloat16)
    nusers = cache_keys.shape[1]
    depth = cache_keys.shape[2]
    keys = jnp.concatenate([cache_keys.reshape(nusers * depth, group_width), key_new], axis=0)
    values = jnp.concatenate([cache_values.reshape(nusers * depth, group_width), value_new], axis=0)
    cached = jnp.arange(nusers * depth, dtype=jnp.int32)
    cache_user = cached // depth
    cache_live = cached % depth < jnp.repeat(cache_len[0], depth)
    cache_ok = (users[:, None] == cache_user[None, :]) & cache_live[None, :]
    order = jnp.arange(slots, dtype=jnp.int32)
    new_ok = (
        (users[:, None] == users[None, :]) & valid[None, :] & (order[None, :] <= order[:, None])
    )
    new_ok = new_ok | (order[:, None] == order[None, :])
    allowed = jnp.concatenate([cache_ok, new_ok], axis=1)
    attn = attend(query, keys, values, allowed, HEAD_DIM)
    partial_terms = jnp.dot(attn, w_out, preferred_element_type=jnp.float32)
    summed = lax.psum(partial_terms.astype(jnp.bfloat16), "heads").astype(jnp.float32)
    mixed = lax.dynamic_slice_in_dim(summed, lax.axis_index("heads") * group_width, group_width, 1)
    updated = jnp.where(
        valid[:, None],
        (got_rows.astype(jnp.float32) + mixed).astype(jnp.bfloat16),
        jnp.zeros((), jnp.bfloat16),
    )
    which = jnp.arange(nusers, dtype=jnp.int32)
    hits = valid[None, :] & (users[None, :] == which[:, None])
    last = jnp.max(jnp.where(hits, order[None, :], -1), axis=1)
    picker = (order[None, :] == last[:, None]).astype(jnp.bfloat16)
    state = jnp.dot(picker, updated, preferred_element_type=jnp.float32).astype(jnp.bfloat16)
    ranks = user_rank[0]
    bound_for = ranks[None, :] == jnp.arange(owners, dtype=jnp.int32)[:, None]
    outgoing = jnp.where(bound_for[:, :, None], state[None, :, :], jnp.zeros((), jnp.bfloat16))
    arrived = lax.all_to_all(
        outgoing.reshape(owners * nusers, group_width),
        "users",
        split_axis=0,
        concat_axis=0,
        tiled=True,
    )
    return (updated[None], arrived[None])


def solution(mesh):
    placed = (
        P("users", "heads"),
        P("users", None),
        P("users"),
        P("users", None, None, "heads"),
        P("users", None, None, "heads"),
        P("users", None),
        P("users", None),
        P(),
        P(None, "heads"),
        P(None, "heads"),
        P(None, "heads"),
        P("heads", None),
    )
    return jax.shard_map(
        local,
        mesh=mesh,
        in_specs=placed,
        out_specs=(P("users", None, "heads"), P("users", None, "heads")),
        check_vma=False,
    )
```

profile of v0, /device:TPU:1, one launch (start us, length us, event | category | flops | bytes accessed | tf_op | source)
XLA Modules:
  0.0 186.8 jit_solution(6484904027811097856)
XLA Ops:
  7.2 0.9 copy.33
  8.4 0.9 fusion.21
  10.0 1.9 %scatter_custom_fusion.1 = bf16[512,256]{1,0:T(8,128)(2,1)S(1)} fusion(s32[256]{0:T(256)S(1)} %bitcast.82, bf16[256,256]{1,0:T(8,128)(2,1)} %param.14, bf16[]{:T(256)} %constant.73.clone.1), kind=kCustom, calls=%fused_computation.45 | custom fusion | bytes 262656 | tf_op jit(solution)/shard_map/scatter | solution.py:52
  12.0 33.6 %all_to_all.27 = bf16[128,4,256]{2,1,0:T(4,128)(2,1)S(1)} all-to-all(bf16[128,4,256]{2,1,0:T(4,128)(2,1)S(1)} %all_to_all.20), channel_id=1, replica_groups=mesh['users'=128,'heads'=4] {'users'}, dimensions={0} | all-to-all | bytes 524288 | tf_op jit(solution)/shard_map/all_to_all | solution.py:55
  45.6 0.8 all_to_all.22
  46.4 1.6 scatter_custom_fusion
  47.9 0.7 all_to_all.18
  48.7 5.5 %all-to-all-start = ((s32[128,4,1]{1,2,0:T(1,128)}), s32[128,4,1]{1,2,0:T(1,128)S(1)}, u32[]{:S(2)}, u32[]{:S(2)}) async-start(s32[128,4,1]{1,2,0:T(1,128)} %bitcast.11), calls=%async_computation | async-start | bytes 131072 | tf_op jit(solution)/shard_map/all_to_all | solution.py:56
  55.9 1.2 concatenate.23
  57.1 8.5 %all-to-all-done = s32[128,4,1]{1,2,0:T(1,128)S(1)} async-done(((s32[128,4,1]{1,2,0:T(1,128)}), s32[128,4,1]{1,2,0:T(1,128)S(1)}, u32[]{:S(2)}, u32[]{:S(2)}) %all-to-all-start) | async-done | bytes 2080 | tf_op jit(solution)/shard_map/all_to_all | solution.py:56
  67.1 2.0 %all-gather.2.cloned.1.call-done = bf16[512,1024]{1,0:T(8,128)(2,1)} async-done(((bf16[512,256]{1,0:T(8,128)(2,1)}), bf16[512,1024]{1,0:T(8,128)(2,1)}) %all-gather.2.cloned.1.call-update) | async-done | bytes 1048592 | tf_op jit(solution)/shard_map/all_gather | solution.py:60
  69.1 1.5 fusion.14
  70.6 2.0 %convolution_convert_fusion.3 = bf16[512,256]{0,1:T(8,128)(2,1)S(1)} fusion(bf16[1024,256]{1,0:T(8,128)(2,1)} %param.22, bf16[512,1024]{1,0:T(8,128)(2,1)} %all-gather.2.cloned.1.call-done, f32[1024]{0:T(1024)S(1)} %copy-done.9, f32[512]{0:T(512)S(1)} %add_rsqrt_fusion), kind=kOutput, calls=%fused_computation.29 | convolution fusion | flops 270663680 | bytes 1841152 | tf_op jit(solution)/shard_map/dot_general | solution.py:65
  72.9 1.9 %convolution_convert_fusion.1 = bf16[512,256]{0,1:T(8,128)(2,1)S(1)} fusion(bf16[1024,256]{1,0:T(8,128)(2,1)S(1)} %copy-done.7, bf16[512,1024]{1,0:T(8,128)(2,1)} %all-gather.2.cloned.1.call-done, f32[1024]{0:T(1024)S(1)} %copy-done.9, f32[512]{0:T(512)S(1)} %add_rsqrt_fusion), kind=kOutput, calls=%fused_computation.27 | convolution fusion | flops 270663680 | bytes 1841152 | tf_op jit(solution)/shard_map/dot_general | solution.py:67
  74.8 1.8 convolution_convert_fusion.2
  76.7 1.0 maximum_bitcast_fusion
  77.6 12.4 %while.10 = (s32[]{:T(128)}, bf16[4,512,64]{1,2,0:T(8,128)(2,1)S(1)}, bf16[4,512,64]{2,1,0:T(8,128)(2,1)S(1)}, bf16[4,1536,64]{1,2,0:T(8,128)(2,1)S(1)}, pred[51...) while((s32[]{:T(128)}, bf16[4,512,64]{1,2,0:T(8,128)(2,1)S(1)}, ...), condition=%wide.region_9.10_spmd, body=%wide.region_6.9_spmd.sunk | while | flops 207649792 | bytes 10825805 | solution.py:26
  77.6 0.7 fusion.56
  78.9 1.8 fusion.58
  80.7 0.7 fusion.56
  82.0 1.8 fusion.58
  83.8 0.7 fusion.56
  85.1 1.8 fusion.58
  86.9 0.7 fusion.56
  88.2 1.8 fusion.58
  90.1 1.5 convolution_convert_fusion
  91.7 57.0 %all-reduce.2.cloned.1.call-done = bf16[512,1024]{1,0:T(8,128)(2,1)} async-done(((bf16[512,1024]{1,0:T(8,128)(2,1)}), bf16[512,1024]{1,0:T(8,128)(2,1)}) %all-reduce.2.cloned.1.call-update) | async-done | bytes 1048592 | tf_op jit(solution)/shard_map/psum | solution.py:84
  148.8 1.2 convolution_convert_fusion.4
  150.0 0.9 broadcast_select_fusion
  150.8 15.7 %all-to-all-start.2 = ((bf16[128,2,256]{2,1,0:T(2,128)(2,1)}), bf16[128,2,256]{2,1,0:T(2,128)(2,1)S(1)}, u32[]{:S(2)}, u32[]{:S(2)}) async-start(bf16[128,2,256]{2,1,0:T(2,128)(2,1)} %broadcast_select_fusion), calls=%async_computation.2 | async-start | bytes 262144 | tf_op jit(solution)/shard_map/all_to_all | solution.py:99
  166.5 1.8 fusion.41
  168.3 10.9 %all-to-all-done.2 = bf16[128,2,256]{2,1,0:T(2,128)(2,1)S(1)} async-done(((bf16[128,2,256]{2,1,0:T(2,128)(2,1)}), bf16[128,2,256]{2,1,0:T(2,128)(2,1)S(1)}, u32[]{:S(2)}, u32[]{:S(2)}) %all-to-all-start.2) | async-done | bytes 131104 | tf_op jit(solution)/shard_map/all_to_all | solution.py:99
  (58 shorter events, 7.6 us)
Async XLA Ops:
  7.2 82.9 %copy-start = (bf16[256,1024]{1,0:T(8,128)(2,1)S(1)}, bf16[256,1024]{1,0:T(8,128)(2,1)}, u32[]{:S(2)}) copy-start(bf16[256,1024]{1,0:T(8,128)(2,1)} %param.25) | copy-start | bytes 1572868
  7.2 47.2 %copy-start.5 = (s32[1,2]{1,0:T(1,128)S(1)}, s32[1,2]{1,0:T(1,128)}, u32[]{:S(2)}) copy-start(s32[1,2]{1,0:T(1,128)} %param.19) | copy-start | bytes 28
  7.2 47.3 %copy-start.3 = (bf16[1,2,512,256]{3,2,1,0:T(8,128)(2,1)S(1)}, bf16[1,2,512,256]{3,2,1,0:T(8,128)(2,1)}, u32[]{:S(2)}) copy-start(bf16[1,2,512,256]{3,2,1,0:T(8,128)(2,1)} %param.17) | copy-start | bytes 1572868
  7.2 61.9 %all-gather.2.cloned.1.call-start = ((), (), s32[]{:S(2)}) async-start(), calls=%async_computation.3 | async-start | bytes 1310720 | tf_op jit(solution)/shard_map/all_gather | solution.py:60
  11.9 43.5 %copy-start.4 = (bf16[1,2,512,256]{3,2,1,0:T(8,128)(2,1)S(1)}, bf16[1,2,512,256]{3,2,1,0:T(8,128)(2,1)}, u32[]{:S(2)}) copy-start(bf16[1,2,512,256]{3,2,1,0:T(8,128)(2,1)} %param.18) | copy-start | bytes 1572868
  48.7 17.0 %all-to-all-start = ((s32[128,4,1]{1,2,0:T(1,128)}), s32[128,4,1]{1,2,0:T(1,128)S(1)}, u32[]{:S(2)}, u32[]{:S(2)}) async-start(s32[128,4,1]{1,2,0:T(1,128)} %bitcast.11), calls=%async_computation | async-start | bytes 131072 | tf_op jit(solution)/shard_map/all_to_all | solution.py:56
  54.2 94.6 %all-reduce.2.cloned.1.call-start = ((), (), s32[]{:S(2)}) async-start(), calls=%async_computation.4 | async-start | bytes 2097152 | tf_op jit(solution)/shard_map/psum | solution.py:84
  57.1 13.4 %copy-start.9 = (f32[1024]{0:T(1024)S(1)}, f32[1024]{0:T(1024)}, u32[]{:S(2)}) copy-start(f32[1024]{0:T(1024)} %param.21) | copy-start | bytes 12292
  67.1 5.8 %copy-start.7 = (bf16[1024,256]{1,0:T(8,128)(2,1)S(1)}, bf16[1024,256]{1,0:T(8,128)(2,1)}, u32[]{:S(2)}) copy-start(bf16[1024,256]{1,0:T(8,128)(2,1)} %param.24) | copy-start | bytes 1572868
  72.8 2.0 %copy-start.8 = (bf16[1024,256]{1,0:T(8,128)(2,1)S(1)}, bf16[1024,256]{1,0:T(8,128)(2,1)}, u32[]{:S(2)}) copy-start(bf16[1024,256]{1,0:T(8,128)(2,1)} %param.23) | copy-start | bytes 1572868
  72.9 3.8 %copy-start.2 = (bf16[1024,4,64]{0,2,1:T(8,128)(2,1)S(1)}, bf16[1024,4,64]{0,2,1:T(8,128)(2,1)}, u32[]{:S(2)}) copy-start(bf16[1024,4,64]{0,2,1:T(8,128)(2,1)} %concatenate.23) | copy-start | bytes 1572868
  90.0 1.6 copy-start.6
  90.0 58.7 %copy-start.1 = (bf16[512,256]{1,0:T(8,128)(2,1)S(1)}, bf16[512,256]{1,0:T(8,128)(2,1)}, u32[]{:S(2)}) copy-start(bf16[512,256]{1,0:T(8,128)(2,1)} %all_to_all.22) | copy-start | bytes 786436
  150.8 28.4 %all-to-all-start.2 = ((bf16[128,2,256]{2,1,0:T(2,128)(2,1)}), bf16[128,2,256]{2,1,0:T(2,128)(2,1)S(1)}, u32[]{:S(2)}, u32[]{:S(2)}) async-start(bf16[128,2,256]{2,1,0:T(2,128)(2,1)} %broadcast_select_fusion), calls=%async_computation.2 | async-start | bytes 262144 | tf_op jit(solution)/shard_map/all_to_all | solution.py:99
Sparse Core Ops, SparseCore 0:
  46.5 22.5 all-gather.1
  91.7 57.0 all-reduce.1
where the time goes:
time: 187 us
  waiting for transfers between devices  78.5 us (42%)
  blocking collectives  33.6 us (18%)
  starting transfers between devices  21.4 us (11%)
  matrix products  18.4 us (10%)
  between operations  14.4 us (8%)
  other arithmetic  10.6 us (6%)
  local copies, waits for them, and re-layouts  9.82 us (5%)
    psum x1, waiting for transfers between devices, local(): lax.psum(partial_terms.astype(jnp.bfloat16), 'heads').astype(jnp.float32)  57 us
    all_to_all x1, blocking collectives, local(): lax.all_to_all(send_rows, 'users', split_axis=0, concat_axis=0, tiled=True)  33.6 us
    all_to_all x1, starting transfers between devices, local(): lax.all_to_all(outgoing.reshape(owners * nusers, group_width), 'users', s...  15.7 us
    all_to_all x1, waiting for transfers between devices, local(): lax.all_to_all(outgoing.reshape(owners * nusers, group_width), 'users', s...  10.9 us
    all_to_all x1, waiting for transfers between devices, local(): lax.all_to_all(send_user, 'users', split_axis=0, concat_axis=0, tiled=True)  8.55 us
    dot_general x4, matrix products, single(): jnp.dot(probs, vpart, preferred_element_type=jnp.float32)  7.1 us
    all_to_all x1, starting transfers between devices, local(): lax.all_to_all(send_user, 'users', split_axis=0, concat_axis=0, tiled=True)  5.51 us
  transfers between devices with their start and end apart: 4, of which 4 were waited for; matrix products, arithmetic and copies ran while one was open for 4% of the time, Pallas kernels for 0%

commit v1 on v0

v1 whole, which is shorter than its diff:
```python
import functools

import jax
import jax.numpy as jnp
from jax import lax
from jax.experimental import pallas as pl
from jax.experimental.pallas import tpu as pltpu
from jax.sharding import PartitionSpec as P

HEAD_DIM = 64
LANES = 128
CHUNK = 10
BIG = 1e30
VMEM = 48 * 1024 * 1024


def iota(shape, axis):
    return lax.broadcasted_iota(jnp.int32, shape, axis)


def route_kernel(owners, cap, owner_ref, user_ref, events_ref, out_ref):
    owner = owner_ref[...]
    user = user_ref[...]
    count = owner.shape[1]
    member = (iota((owners, count), 0) == owner).astype(jnp.bfloat16)
    same = lax.dot_general(member, member, (((0,), (0,)), ((), ())), preferred_element_type=jnp.float32)
    earlier = iota((count, count), 0) < iota((count, count), 1)
    rank = jnp.sum(jnp.where(earlier, same, 0.0), axis=0, keepdims=True).astype(jnp.int32)
    target = owner * CHUNK + rank
    line = iota((owners * CHUNK, 1), 0)
    dest = jnp.floor((line.astype(jnp.float32) + 0.5) * (1.0 / CHUNK)).astype(jnp.int32)
    part = line - dest * CHUNK
    slot = jnp.where(part >= cap, part - cap, part)
    slot_line = jnp.where(part < 2 * cap, dest * CHUNK + slot, -1)
    user_line = jnp.where(part == 2 * cap, dest, -1)
    pick = jnp.where((slot_line == target) | (user_line == owner), 1.0, 0.0).astype(jnp.bfloat16)
    rows = jnp.dot(pick, events_ref[...], preferred_element_type=jnp.float32)
    named = jnp.where(iota((LANES, count), 0) == rank, user + 1, 0).astype(jnp.float32).astype(jnp.bfloat16)
    users = lax.dot_general(pick, named, (((1,), (1,)), ((), ())), preferred_element_type=jnp.float32) - 1.0
    value = jnp.where(part < cap, rows[:, :LANES], rows[:, LANES:])
    value = jnp.where(part < 2 * cap, value, jnp.where(part == 2 * cap, users, 0.0))
    out_ref[...] = value.astype(jnp.bfloat16)


def attend_kernel(
    rows_ref, meta_ref, len_ref, gain_ref, wq_ref, wk_ref, wv_ref, ck_ref, cv_ref, wo_ref,
    out_ref, normed_ref, query_ref, key_ref, value_ref, attn_ref,
):
    groups, parts, sources, _ = rows_ref.shape
    cap = parts // 2
    slots = cap * sources
    depth = ck_ref.shape[1]
    cached = 2 * depth
    for k in range(cap):
        wide = jnp.concatenate(
            [rows_ref[g, half * cap + k] for g in range(groups) for half in range(2)], axis=1
        ).astype(jnp.float32)
        mean = jnp.mean(wide * wide, axis=1, keepdims=True)
        normed = wide * lax.rsqrt(mean + 1e-05) * gain_ref[...]
        normed_ref[k * sources:(k + 1) * sources, :] = normed.astype(jnp.bfloat16)
    normed = normed_ref[...]
    query = jnp.dot(normed, wq_ref[...], preferred_element_type=jnp.float32).astype(jnp.bfloat16)
    query_ref[...] = query * jnp.bfloat16(HEAD_DIM ** -0.5)
    key_ref[...] = jnp.dot(normed, wk_ref[...], preferred_element_type=jnp.float32).astype(jnp.bfloat16)
    value_ref[...] = jnp.dot(normed, wv_ref[...], preferred_element_type=jnp.float32).astype(jnp.bfloat16)

    users = jnp.concatenate([meta_ref[:, k:k + 1] for k in range(cap)], axis=0).astype(jnp.float32)
    place = iota((cached, 1), 0)
    first = place < depth
    limit = jnp.where(first, len_ref[0, 0], len_ref[0, 1] + depth)
    cache_user = jnp.where(place < limit, jnp.where(first, 0.0, 1.0), -1.0)
    key_user = jnp.concatenate([cache_user, users], axis=0)
    lane = iota((1, LANES), 1)
    total = cached + slots
    row = iota((sources, sources), 0)
    col = iota((sources, sources), 1)
    upto = jnp.where(col <= row, 0.0, -BIG)
    under = jnp.where(col < row, 0.0, -BIG)
    for side in range(2):
        inside = lane // HEAD_DIM == side
        inside_one = jnp.where(inside, 1.0, 0.0).astype(jnp.bfloat16)
        outside_one = jnp.where(inside, 0.0, 1.0).astype(jnp.bfloat16)
        base = HEAD_DIM * (1 - side)
        wrong = jnp.where(lane == base, jnp.where(key_user == 0.0, 0.0, -BIG), 0.0)
        wrong = wrong + jnp.where(lane == base + 1, jnp.where(key_user == 1.0, 0.0, -BIG), 0.0)
        wrong = wrong.astype(jnp.bfloat16)
        asks = jnp.where(lane == base, jnp.where(users == 1.0, 0.0, 1.0), 0.0)
        asks = asks + jnp.where(lane == base + 1, jnp.where(users == 1.0, 1.0, 0.0), 0.0)
        asks = asks.astype(jnp.bfloat16)
        for pair in range(2):
            at = slice(pair * LANES, (pair + 1) * LANES)
            keys = jnp.concatenate([ck_ref[0, :, at], ck_ref[1, :, at], key_ref[:, at]], axis=0)
            keys = keys * inside_one + wrong
            values = jnp.concatenate([cv_ref[0, :, at], cv_ref[1, :, at], value_ref[:, at]], axis=0)
            values = values * inside_one + outside_one
            queries = query_ref[:, at] * inside_one + asks
            for k in range(cap):
                rows = slice(k * sources, (k + 1) * sources)
                scores = lax.dot_general(
                    queries[rows], keys, (((1,), (1,)), ((), ())), preferred_element_type=jnp.float32
                )
                bias = jnp.concatenate([upto if other <= k else under for other in range(cap)], axis=1)
                fresh = scores[:, cached:] + bias
                old = scores[:, :cached]
                top = jnp.maximum(jnp.max(old, axis=1, keepdims=True), jnp.max(fresh, axis=1, keepdims=True))
                weights = jnp.concatenate(
                    [jnp.exp(old - top).astype(jnp.bfloat16), jnp.exp(fresh - top).astype(jnp.bfloat16)], axis=1
                )
                mixed = jnp.dot(weights, values, preferred_element_type=jnp.float32)
                mixed = (mixed / pltpu.roll(mixed, HEAD_DIM, 1)).astype(jnp.bfloat16)
                here = slice(pair * LANES + side * HEAD_DIM, pair * LANES + (side + 1) * HEAD_DIM)
                attn_ref[rows, here] = mixed[:, side * HEAD_DIM:(side + 1) * HEAD_DIM]
    attn = attn_ref[...]
    width = out_ref.shape[2]
    for g in range(groups):
        out_ref[g] = jnp.dot(
            attn, wo_ref[:, g * width:(g + 1) * width], preferred_element_type=jnp.float32
        ).astype(jnp.bfloat16)


def state_kernel(owners, rank_ref, meta_ref, rows_ref, terms_ref, out_ref):
    groups, slots, width = terms_ref.shape
    sources = meta_ref.shape[0]
    cap = slots // sources
    source = iota((sources, 1), 0)
    lines = []
    for user in range(2):
        last = jnp.full((1, 1), -1, jnp.int32)
        for k in range(cap):
            hit = meta_ref[:, k:k + 1].astype(jnp.float32) == user
            best = jnp.max(jnp.where(hit, source * cap + k, -1), axis=0, keepdims=True)
            last = jnp.maximum(last, best)
        lines.append(last)
    lane = iota((1, sources), 1)
    which = iota((8, 1), 0)
    last = jnp.where(which == 0, lines[0], jnp.where(which == 1, lines[1], -1))
    mixed = jnp.zeros((8, width), jnp.float32)
    base = jnp.zeros((8, width), jnp.float32)
    for k in range(cap):
        pick = jnp.where(lane * cap + k == last, 1.0, 0.0).astype(jnp.bfloat16)
        for g in range(groups):
            mixed = mixed + jnp.dot(
                pick, terms_ref[g, k * sources:(k + 1) * sources, :], preferred_element_type=jnp.float32
            )
        own = jnp.concatenate([rows_ref[k], rows_ref[cap + k]], axis=1)
        base = base + jnp.dot(pick, own, preferred_element_type=jnp.float32)
    state = base + mixed
    line = iota((owners * 4, 1), 0)
    dest, part = line >> 2, line & 3
    value = jnp.zeros((owners * 4, LANES), jnp.float32)
    for user in range(2):
        for half in range(2):
            mine = (part == user * 2 + half) & (dest == rank_ref[0, user])
            value = jnp.where(mine, state[user:user + 1, half * LANES:(half + 1) * LANES], value)
    out_ref[...] = value.astype(jnp.bfloat16)


def call(kernel, out, args, scratch=(), smem=(), cost=None):
    specs = [pl.BlockSpec(memory_space=pltpu.SMEM if i in smem else pltpu.VMEM) for i in range(len(args))]
    return pl.pallas_call(
        kernel,
        out_shape=out,
        in_specs=specs,
        out_specs=pl.BlockSpec(memory_space=pltpu.VMEM),
        scratch_shapes=list(scratch),
        cost_estimate=cost,
        compiler_params=pltpu.CompilerParams(vmem_limit_bytes=VMEM),
    )(*args)


def local(
    events, event_owner, event_user, cache_keys, cache_values, cache_len, user_rank,
    norm_gain, w_query, w_key, w_value, w_out,
):
    count, width = events.shape
    owners = lax.axis_size("users")
    groups = lax.axis_size("heads")
    cap = 2 * count // owners
    slots = owners * cap
    bf16 = jnp.bfloat16
    sent = call(
        functools.partial(route_kernel, owners, cap),
        jax.ShapeDtypeStruct((owners * CHUNK, LANES), bf16),
        (event_owner.reshape(1, count), event_user.reshape(1, count), events),
    )
    got = lax.all_to_all(
        sent.reshape(owners, CHUNK // 2, 2, LANES), "users", split_axis=0, concat_axis=0, tiled=True
    )
    got = got.reshape(owners, CHUNK, LANES).transpose(1, 0, 2)
    own, meta = got[:2 * cap], got[2 * cap]
    full = lax.all_to_all(
        jnp.broadcast_to(own, (groups,) + own.shape), "heads", split_axis=0, concat_axis=0, tiled=True
    )
    terms = call(
        attend_kernel,
        jax.ShapeDtypeStruct((groups, slots, width), bf16),
        (
            full, meta, cache_len, norm_gain.reshape(1, -1), w_query, w_key, w_value,
            cache_keys[0], cache_values[0], w_out,
        ),
        scratch=[
            pltpu.VMEM((slots, groups * width), bf16),
            pltpu.VMEM((slots, width), bf16),
            pltpu.VMEM((slots, width), bf16),
            pltpu.VMEM((slots, width), bf16),
            pltpu.VMEM((slots, width), bf16),
        ],
        smem=(2,),
    )
    terms = lax.all_to_all(terms, "heads", split_axis=0, concat_axis=0, tiled=True)
    outgoing = call(
        functools.partial(state_kernel, owners),
        jax.ShapeDtypeStruct((owners * 4, LANES), bf16),
        (user_rank, meta, own, terms),
        smem=(0,),
    )
    arrived = lax.all_to_all(
        outgoing.reshape(owners, 4, LANES), "users", split_axis=0, concat_axis=0, tiled=True
    )
    ranked = arrived.reshape(1, owners * 2, width)

    mixed = jnp.sum(terms.astype(jnp.float32), axis=0).reshape(cap, owners, width)
    base = own.reshape(2, cap, owners, LANES).transpose(1, 2, 0, 3).reshape(cap, owners, width)
    valid = meta[:, :cap].T >= 0
    updated = jnp.where(valid[:, :, None], (base.astype(jnp.float32) + mixed).astype(bf16), jnp.zeros((), bf16))
    refreshed = updated.transpose(1, 0, 2).reshape(1, slots, width)
    return refreshed, ranked


def solution(mesh):
    placed = (
        P("users", "heads"),
        P("users", None),
        P("users"),
        P("users", None, None, "heads"),
        P("users", None, None, "heads"),
        P("users", None),
        P("users", None),
        P(),
        P(None, "heads"),
        P(None, "heads"),
        P(None, "heads"),
        P("heads", None),
    )
    return jax.shard_map(
        local,
        mesh=mesh,
        in_specs=placed,
        out_specs=(P("users", None, "heads"), P("users", None, "heads")),
        check_vma=False,
    )
```

time: 187 us -> 112 us (0.60)
  waiting for transfers between devices: 78.5 us -> 38.7 us
  matrix products: 18.4 us -> 0 us
  between operations: 14.4 us -> 0.78 us
  Pallas kernels: 0 us -> 12.8 us
  other arithmetic: 10.6 us -> 0.22 us
  starting transfers between devices: 21.4 us -> 15.3 us
    psum x1 -> x0, waiting for transfers between devices: 57 us -> none  [local(): lax.psum(partial_terms.astype(jnp.bfloat16), 'heads').astype(jnp.float32)]
    all_to_all x2 -> x3, waiting for transfers between devices: 19.5 us -> 38.7 us  [the longest x1 13.9 us: local(): lax.all_to_all(jnp.broadcast_to(own, (groups,) + own.shape), 'heads', spl...]
    dot_general x13 -> x0, matrix products: 18.4 us -> none  [the longest x4 7.1 us: single(): jnp.dot(probs, vpart, preferred_element_type=jnp.float32)]
    pallas_call x0 -> x3, Pallas kernels: none -> 12.8 us  [call(): pl.pallas_call(kernel, out_shape=out, in_specs=specs, out_specs=pl.BlockS...]
    all_to_all x2 -> x3, starting transfers between devices: 21.2 us -> 15.3 us  [the longest x1 7.52 us: local(): lax.all_to_all(outgoing.reshape(owners, 4, LANES), 'users', split_axis=0,...]
    reduce_sum x6 -> x1, other arithmetic: 4.66 us -> 0.14 us  [local(): jnp.sum(terms.astype(jnp.float32), axis=0).reshape(cap, owners, width)]
    unnamed x25 -> x26, local copies, waits for them, and re-layouts: 1.16 us -> 5.1 us
    scatter x2 -> x0, local copies, waits for them, and re-layouts: 3.46 us -> none  [the longest x1 1.9 us: local(): jnp.zeros((slots, group_width), jnp.bfloat16).at[target].set(events)]
  transfers between devices with their start and end apart: 4 -> 3, of which waited for: 4 -> 3; matrix products, arithmetic and copies ran while one was open for 4% -> 2% of each run, Pallas kernels for 0% -> 0%
where the time goes in v1:
time: 112 us
  waiting for transfers between devices  38.7 us (35%)
  blocking collectives  34.8 us (31%)
  starting transfers between devices  15.3 us (14%)
  Pallas kernels  12.8 us (11%)
  local copies, waits for them, and re-layouts  9.25 us (8%)
    all_to_all x1, blocking collectives, local(): lax.all_to_all(sent.reshape(owners, CHUNK // 2, 2, LANES), 'users', split...  34.8 us
    all_to_all x1, waiting for transfers between devices, local(): lax.all_to_all(jnp.broadcast_to(own, (groups,) + own.shape), 'heads', spl...  13.9 us
    all_to_all x1, waiting for transfers between devices, local(): lax.all_to_all(terms, 'heads', split_axis=0, concat_axis=0, tiled=True)  13.4 us
    pallas_call x3, Pallas kernels, call(): pl.pallas_call(kernel, out_shape=out, in_specs=specs, out_specs=pl.BlockS...  12.8 us
    all_to_all x1, waiting for transfers between devices, local(): lax.all_to_all(outgoing.reshape(owners, 4, LANES), 'users', split_axis=0,...  11.5 us
    all_to_all x1, starting transfers between devices, local(): lax.all_to_all(outgoing.reshape(owners, 4, LANES), 'users', split_axis=0,...  7.52 us
    unnamed x26, local copies, waits for them, and re-layouts  5.1 us
    all_to_all x1, starting transfers between devices, local(): lax.all_to_all(jnp.broadcast_to(own, (groups,) + own.shape), 'heads', spl...  4.16 us
  transfers between devices with their start and end apart: 3, of which 3 were waited for; matrix products, arithmetic and copies ran while one was open for 2% of the time, Pallas kernels for 0%

profile of v1, /device:TPU:1, one launch (start us, length us, event | category | flops | bytes accessed | tf_op | source)
XLA Modules:
  0.0 111.9 jit_solution(1371713186194768098)
XLA Ops:
  0.6 0.0 copy-start.6
  0.6 0.9 copy-done.6
  1.5 0.7 copy-done.8
  2.2 0.7 copy-done.9
  2.9 1.0 shard_map.131
  3.9 34.8 %all_to_all.20 = bf16[128,5,2,128]{3,2,1,0:T(2,128)(2,1)S(1)} all-to-all(bf16[128,5,2,128]{3,2,1,0:T(2,128)(2,1)S(1)} %bitcast.27), channel_id=1, replica_groups=mesh['users'=128,'heads'=4] {'users'}, dimensions={0} | all-to-all | bytes 655360 | tf_op jit(solution)/shard_map/all_to_all | solution.py:186
  38.7 0.0 copy-start.12
  38.7 0.7 copy-done.12
  39.5 1.2 %broadcast_in_dim.17 = bf16[4,8,128,128]{3,2,1,0:T(8,128)(2,1)} broadcast(bf16[8,128,128]{2,1,0:T(8,128)(2,1)S(1)} %slice.14.rows_ref), dimensions={1,2,3} | broadcast | bytes 1310720 | tf_op jit(solution)/shard_map/broadcast_in_dim | solution.py:192
  40.7 0.0 copy-start.7
  40.7 0.0 copy-start.10
  40.7 4.2 %all-to-all-start.1 = ((bf16[4,8,128,128]{3,2,1,0:T(8,128)(2,1)}), bf16[4,8,128,128]{3,2,1,0:T(8,128)(2,1)S(1)}, u32[]{:S(2)}, u32[]{:S(2)}) async-start(bf16[4,8,128,128]{3,2,1,0:T(8,128)(2,1)} %broadcast_in_dim.17), calls=%async_computation.1 | async-start | bytes 2097152 | tf_op jit(solution)/shard_map/all_to_all | solution.py:191
  44.9 0.8 slice_bitcast_fusion.meta_ref
  45.7 13.9 %all-to-all-done.1.rows_ref = bf16[4,8,128,128]{3,2,1,0:T(8,128)(2,1)S(1)} async-done(((bf16[4,8,128,128]{3,2,1,0:T(8,128)(2,1)}), bf16[4,8,128,128]{3,2,1,0:T(8,128)(2,1)S(1)}, u32[]{:S(2)}, u32[]{:S(2)}) %all-to-all-start.1) | async-done | bytes 1048608 | tf_op jit(solution)/shard_map/all_to_all | solution.py:191
  59.5 0.0 copy-done.1
  59.6 0.0 copy-start.4
  59.6 1.0 copy-done.4
  60.6 1.0 copy-done.5
  61.6 9.9 %shard_map.132 = bf16[4,512,256]{2,1,0:T(8,128)(2,1)} custom-call(bf16[4,8,128,128]{3,2,1,0:T(8,128)(2,1)S(1)} %all-to-all-done.1.rows_ref, bf16[128,128]{1,0:T(8,128)(2,1)S(1)} %slice_bitcast_fusion.meta_ref, s32[1,2]{1,0:T(1,128)S(1)} %copy-done.10, f32[1,1024]{1,0:T(1,128)S(1)} %bitcast.30, bf16[1024,256]{1,0:T(8,128)(2,1)S(1)} %copy-done, ...), custom_call_target="tpu_custom_call" | custom-call | tf_op jit(solution)/shard_map/pallas_call | solution.py:160
  71.6 3.6 %all-to-all-start.2 = ((bf16[4,512,256]{2,1,0:T(8,128)(2,1)}), bf16[4,512,256]{2,1,0:T(8,128)(2,1)S(1)}, u32[]{:S(2)}, u32[]{:S(2)}) async-start(bf16[4,512,256]{2,1,0:T(8,128)(2,1)} %shard_map.132), calls=%async_computation.2 | async-start | bytes 2097152 | tf_op jit(solution)/shard_map/all_to_all | solution.py:210
  75.2 0.1 copy.26
  75.4 0.1 copy.25
  75.5 13.4 %all-to-all-done.2.terms_ref = bf16[4,512,256]{2,1,0:T(8,128)(2,1)S(1)} async-done(((bf16[4,512,256]{2,1,0:T(8,128)(2,1)}), bf16[4,512,256]{2,1,0:T(8,128)(2,1)S(1)}, u32[]{:S(2)}, u32[]{:S(2)}) %all-to-all-start.2) | async-done | bytes 1048608 | tf_op jit(solution)/shard_map/all_to_all | solution.py:210
  88.9 1.8 %shard_map.133 = bf16[512,128]{1,0:T(8,128)(2,1)} custom-call(s32[1,2]{1,0:T(1,128)S(1)} %copy-done.11, bf16[128,128]{1,0:T(8,128)(2,1)S(1)} %slice_bitcast_fusion.meta_ref, bf16[8,128,128]{2,1,0:T(8,128)(2,1)S(1)} %slice.14.rows_ref, bf16[4,512,256]{2,1,0:T(8,128)(2,1)S(1)} %all-to-all-done.2.terms_ref), custom_call_target="tpu_custom_call" | custom-call | tf_op jit(solution)/shard_map/pallas_call | solution.py:160
  90.8 7.5 %all-to-all-start.3 = ((bf16[128,4,128]{2,1,0:T(4,128)(2,1)}), bf16[128,4,128]{2,1,0:T(4,128)(2,1)S(1)}, u32[]{:S(2)}, u32[]{:S(2)}) async-start(bf16[128,4,128]{2,1,0:T(4,128)(2,1)} %bitcast.16), calls=%async_computation.3 | async-start | bytes 262144 | tf_op jit(solution)/shard_map/all_to_all | solution.py:217
  98.3 0.1 convert_reduce_fusion
  98.4 0.2 copy.27
  98.6 0.1 fusion.1
  98.7 0.2 copy.28
  98.9 0.8 reshape.44
  99.7 11.5 %all-to-all-done.3 = bf16[128,4,128]{2,1,0:T(4,128)(2,1)S(1)} async-done(((bf16[128,4,128]{2,1,0:T(4,128)(2,1)}), bf16[128,4,128]{2,1,0:T(4,128)(2,1)S(1)}, u32[]{:S(2)}, u32[]{:S(2)}) %all-to-all-start.3) | async-done | bytes 131104 | tf_op jit(solution)/shard_map/all_to_all | solution.py:217
  111.1 0.7 reshape.46
  (17 shorter events, 0.1 us)
Async XLA Ops:
  0.6 0.9 copy-start.6
  1.5 0.7 copy-start.8
  2.2 0.7 copy-start.9
  38.7 0.7 copy-start.12
  40.7 18.8 %copy-start = (bf16[1024,256]{1,0:T(8,128)(2,1)S(1)}, bf16[1024,256]{1,0:T(8,128)(2,1)}, u32[]{:S(2)}) copy-start(bf16[1024,256]{1,0:T(8,128)(2,1)} %wq_ref.1) | copy-start | bytes 1572868
  40.7 18.8 %copy-start.1 = (bf16[1024,256]{1,0:T(8,128)(2,1)S(1)}, bf16[1024,256]{1,0:T(8,128)(2,1)}, u32[]{:S(2)}) copy-start(bf16[1024,256]{1,0:T(8,128)(2,1)} %wk_ref.1) | copy-start | bytes 1572868
  40.7 18.8 %copy-start.2 = (bf16[1024,256]{1,0:T(8,128)(2,1)S(1)}, bf16[1024,256]{1,0:T(8,128)(2,1)}, u32[]{:S(2)}) copy-start(bf16[1024,256]{1,0:T(8,128)(2,1)} %wv_ref.1) | copy-start | bytes 1572868
  40.7 18.8 %copy-start.3 = (bf16[1,2,512,256]{3,2,1,0:T(8,128)(2,1)S(1)}, bf16[1,2,512,256]{3,2,1,0:T(8,128)(2,1)}, u32[]{:S(2)}) copy-start(bf16[1,2,512,256]{3,2,1,0:T(8,128)(2,1)} %param.15) | copy-start | bytes 1572868
  40.7 18.8 %copy-start.7 = (f32[1024]{0:T(1024)S(1)}, f32[1024]{0:T(1024)}, u32[]{:S(2)}) copy-start(f32[1024]{0:T(1024)} %param.19) | copy-start | bytes 12292
  40.7 18.8 %copy-start.10 = (s32[1,2]{1,0:T(1,128)S(1)}, s32[1,2]{1,0:T(1,128)}, u32[]{:S(2)}) copy-start(s32[1,2]{1,0:T(1,128)} %len_ref.1) | copy-start | bytes 28
  40.7 18.8 %all-to-all-start.1 = ((bf16[4,8,128,128]{3,2,1,0:T(8,128)(2,1)}), bf16[4,8,128,128]{3,2,1,0:T(8,128)(2,1)S(1)}, u32[]{:S(2)}, u32[]{:S(2)}) async-start(bf16[4,8,128,128]{3,2,1,0:T(8,128)(2,1)} %broadcast_in_dim.17), calls=%async_computation.1 | async-start | bytes 2097152 | tf_op jit(solution)/shard_map/all_to_all | solution.py:191
  59.6 1.0 copy-start.4
  60.6 1.0 copy-start.5
  71.6 17.3 %copy-start.11 = (s32[1,2]{1,0:T(1,128)S(1)}, s32[1,2]{1,0:T(1,128)}, u32[]{:S(2)}) copy-start(s32[1,2]{1,0:T(1,128)} %rank_ref.1) | copy-start | bytes 28
  71.6 17.3 %all-to-all-start.2 = ((bf16[4,512,256]{2,1,0:T(8,128)(2,1)}), bf16[4,512,256]{2,1,0:T(8,128)(2,1)S(1)}, u32[]{:S(2)}, u32[]{:S(2)}) async-start(bf16[4,512,256]{2,1,0:T(8,128)(2,1)} %shard_map.132), calls=%async_computation.2 | async-start | bytes 2097152 | tf_op jit(solution)/shard_map/all_to_all | solution.py:210
  90.8 20.4 %all-to-all-start.3 = ((bf16[128,4,128]{2,1,0:T(4,128)(2,1)}), bf16[128,4,128]{2,1,0:T(4,128)(2,1)S(1)}, u32[]{:S(2)}, u32[]{:S(2)}) async-start(bf16[128,4,128]{2,1,0:T(4,128)(2,1)} %bitcast.16), calls=%async_computation.3 | async-start | bytes 262144 | tf_op jit(solution)/shard_map/all_to_all | solution.py:217

commit v2 on v1

v2 whole, which is shorter than its diff:
```python
import functools

import jax
import jax.numpy as jnp
from jax import lax
from jax.experimental import pallas as pl
from jax.experimental.pallas import tpu as pltpu
from jax.sharding import PartitionSpec as P

HEAD_DIM = 64
LANES = 128
CHUNK = 10
BIG = 1e30
LAST_FLOPS = 30_000_000_000
STEP = 2
EDGE = 16
VMEM = 16 * 1024 * 1024


def iota(shape, axis):
    return lax.broadcasted_iota(jnp.int32, shape, axis)


def route_kernel(owners, cap, owner_hbm, user_hbm, events_hbm, out_ref, owner_ref, user_ref, events_ref, sems):
    copies = [
        pltpu.make_async_copy(source, target, sems.at[i])
        for i, (source, target) in enumerate(
            [(owner_hbm, owner_ref), (user_hbm, user_ref), (events_hbm, events_ref)]
        )
    ]
    for copy in copies:
        copy.start()
    copies[0].wait()
    copies[1].wait()
    owner = owner_ref[...]
    user = user_ref[...]
    count = owner.shape[1]
    member = (iota((owners, count), 0) == owner).astype(jnp.bfloat16)
    same = lax.dot_general(member, member, (((0,), (0,)), ((), ())), preferred_element_type=jnp.float32)
    earlier = iota((count, count), 0) < iota((count, count), 1)
    rank = jnp.sum(jnp.where(earlier, same, 0.0), axis=0, keepdims=True).astype(jnp.int32)
    target = owner * CHUNK + rank
    line = iota((owners * CHUNK, 1), 0)
    dest = jnp.floor((line.astype(jnp.float32) + 0.5) * (1.0 / CHUNK)).astype(jnp.int32)
    part = line - dest * CHUNK
    slot = jnp.where(part >= cap, part - cap, part)
    slot_line = jnp.where(part < 2 * cap, dest * CHUNK + slot, -1)
    user_line = jnp.where(part == 2 * cap, dest, -1)
    pick = jnp.where((slot_line == target) | (user_line == owner), 1.0, 0.0).astype(jnp.bfloat16)
    copies[2].wait()
    rows = jnp.dot(pick, events_ref[...], preferred_element_type=jnp.float32)
    named = jnp.where(iota((LANES, count), 0) == rank, user + 1, 0).astype(jnp.float32).astype(jnp.bfloat16)
    users = lax.dot_general(pick, named, (((1,), (1,)), ((), ())), preferred_element_type=jnp.float32) - 1.0
    value = jnp.where(part < cap, rows[:, :LANES], rows[:, LANES:])
    value = jnp.where(part < 2 * cap, value, jnp.where(part == 2 * cap, users, 0.0))
    out_ref[...] = value.astype(jnp.bfloat16)


def attend_kernel(
    rows_ref, got_ref, len_ref, gain_ref, wq_ref, wk_ref, wv_ref, ck_ref, cv_ref, wo_ref,
    own_ref, next_ref, across_ref, prev_ref, edge_ref, base_ref, normed_ref, query_ref, key_ref, value_ref, attn_ref,
):
    groups, parts, sources, _ = rows_ref.shape
    cap = parts // 2
    slots = cap * sources
    depth = ck_ref.shape[1]
    for k in range(cap):
        wide = jnp.concatenate(
            [rows_ref[g, half * cap + k] for g in range(groups) for half in range(2)], axis=1
        ).astype(jnp.float32)
        mean = jnp.mean(wide * wide, axis=1, keepdims=True)
        normed = wide * lax.rsqrt(mean + 1e-05) * gain_ref[...]
        normed_ref[k * sources:(k + 1) * sources, :] = normed.astype(jnp.bfloat16)
    normed = normed_ref[...]
    query = jnp.dot(normed, wq_ref[...], preferred_element_type=jnp.float32).astype(jnp.bfloat16)
    query_ref[...] = query * jnp.bfloat16(HEAD_DIM ** -0.5)
    key_ref[...] = jnp.dot(normed, wk_ref[...], preferred_element_type=jnp.float32).astype(jnp.bfloat16)
    value_ref[...] = jnp.dot(normed, wv_ref[...], preferred_element_type=jnp.float32).astype(jnp.bfloat16)

    meta = got_ref[2 * cap].astype(jnp.float32)
    users = jnp.concatenate([meta[:, k:k + 1] for k in range(cap)], axis=0)
    second = jnp.where(users == 1.0, 1.0, 0.0)
    lane = iota((1, LANES), 1)
    low = lane < HEAD_DIM
    low_one = jnp.where(low, 1.0, 0.0).astype(jnp.bfloat16)
    high_one = jnp.where(low, 0.0, 1.0).astype(jnp.bfloat16)
    asks = jnp.where(lane == 0, 1.0 - second, jnp.where(lane == 1, second, 0.0)).astype(jnp.bfloat16)
    place = iota((depth, 1), 0)
    wrong_old = jnp.where(
        lane == 0,
        jnp.where(place < len_ref[0, 0], 0.0, -BIG),
        jnp.where(lane == 1, jnp.where(place < len_ref[0, 1], 0.0, -BIG), 0.0),
    )
    wrong_new = jnp.where(
        lane == 0,
        jnp.where(users == 0.0, 0.0, -BIG),
        jnp.where(lane == 1, jnp.where(users == 1.0, 0.0, -BIG), 0.0),
    )
    wrong = jnp.concatenate([wrong_old, wrong_new], axis=0).astype(jnp.bfloat16)
    ones = jnp.ones((depth + slots, LANES), jnp.bfloat16)
    row = iota((sources, sources), 0)
    col = iota((sources, sources), 1)
    upto = jnp.where(col <= row, 0.0, -BIG)
    under = jnp.where(col < row, 0.0, -BIG)
    for pair in range(2):
        at = slice(pair * LANES, (pair + 1) * LANES)
        q, k_new, v_new = query_ref[:, at], key_ref[:, at], value_ref[:, at]
        k_one, v_one = ck_ref[0, :, at], cv_ref[0, :, at]
        q_turn, k_turn, v_turn = (pltpu.roll(x, HEAD_DIM, 1) for x in (q, k_new, v_new))
        k_two, v_two = pltpu.roll(ck_ref[1, :, at], HEAD_DIM, 1), pltpu.roll(cv_ref[1, :, at], HEAD_DIM, 1)
        for side in range(2):
            mine, other = (low_one, high_one) if side == 0 else (high_one, low_one)
            in_mine, in_other = (low, ~low) if side == 0 else (~low, low)
            held = jnp.where(in_mine, 1.0 - second, second).astype(jnp.bfloat16)
            queries = jnp.concatenate([(q * mine + q_turn * other) * held, asks], axis=1)
            keys = jnp.concatenate([k_one * mine + k_two * other, k_new * mine + k_turn * other], axis=0)
            keys = jnp.concatenate([keys, wrong], axis=1)
            values = jnp.concatenate([v_one * mine + v_two * other, v_new * mine + v_turn * other], axis=0)
            values = jnp.concatenate([values, ones], axis=1)
            for t in range(0, cap, STEP):
                rows = slice(t * sources, (t + STEP) * sources)
                scores = lax.dot_general(
                    queries[rows], keys, (((1,), (1,)), ((), ())), preferred_element_type=jnp.float32
                )
                bias = jnp.concatenate(
                    [
                        jnp.concatenate([upto if o <= k else under for o in range(cap)], axis=1)
                        for k in range(t, t + STEP)
                    ],
                    axis=0,
                )
                old, fresh = scores[:, :depth], scores[:, depth:] + bias
                top = jnp.maximum(jnp.max(old, axis=1, keepdims=True), jnp.max(fresh, axis=1, keepdims=True))
                weights = jnp.concatenate(
                    [jnp.exp(old - top).astype(jnp.bfloat16), jnp.exp(fresh - top).astype(jnp.bfloat16)], axis=1
                )
                mixed = jnp.dot(weights, values, preferred_element_type=jnp.float32)
                mixed, total = mixed[:, :LANES], mixed[:, LANES:]
                turned = pltpu.roll(mixed, HEAD_DIM, 1)
                mixed = jnp.where(second[rows] == 1.0, turned, mixed) / total
                here = slice(pair * LANES + side * HEAD_DIM, pair * LANES + (side + 1) * HEAD_DIM)
                attn_ref[rows, here] = mixed[:, side * HEAD_DIM:(side + 1) * HEAD_DIM].astype(jnp.bfloat16)
    attn = attn_ref[...]
    width = own_ref.shape[1]
    source = iota((sources, 1), 0)
    lane_source = iota((1, sources), 1)
    which = iota((EDGE, 1), 0)
    last = jnp.full((EDGE, 1), -1, jnp.int32)
    for user in range(2):
        for k in range(cap):
            hit = jnp.where(meta[:, k:k + 1] == user, source * cap + k, -1)
            best = jnp.max(hit, axis=0, keepdims=True)
            last = jnp.where(which == user, jnp.maximum(last, best), last)
    picks = [
        jnp.where(lane_source * cap + k == last, 1.0, 0.0).astype(jnp.bfloat16) for k in range(cap)
    ]
    base = jnp.zeros((EDGE, width), jnp.float32)
    for k in range(cap):
        own = jnp.concatenate([got_ref[k], got_ref[cap + k]], axis=1)
        base = base + jnp.dot(picks[k], own, preferred_element_type=jnp.float32)
    base_ref[...] = base
    final = jnp.dot(jnp.concatenate(picks, axis=1), attn, preferred_element_type=jnp.float32).astype(jnp.bfloat16)
    me = lax.axis_index("heads")
    for shift, out_ref in enumerate((own_ref, next_ref, across_ref, prev_ref)):
        group = lax.rem(me + shift, groups)
        part = wo_ref[:, pl.ds(pl.multiple_of(group * width, width), width)]
        out_ref[...] = jnp.dot(attn, part, preferred_element_type=jnp.float32).astype(jnp.bfloat16)
        edge_ref[group] = jnp.dot(final, part, preferred_element_type=jnp.float32).astype(jnp.bfloat16)


def state_kernel(owners, rank_ref, base_ref, terms_ref, out_ref):
    state = base_ref[...]
    for g in range(terms_ref.shape[0]):
        state = state + terms_ref[g].astype(jnp.float32)
    line = iota((owners * 4, 1), 0)
    dest, part = line >> 2, line & 3
    value = jnp.zeros((owners * 4, LANES), jnp.float32)
    for user in range(2):
        for half in range(2):
            mine = (part == user * 2 + half) & (dest == rank_ref[0, user])
            value = jnp.where(mine, state[user:user + 1, half * LANES:(half + 1) * LANES], value)
    out_ref[...] = value.astype(jnp.bfloat16)


def ranked_kernel(arrived_ref, out_ref):
    count = out_ref.shape[0]
    line = iota((1, 2 * count), 1)
    row = iota((count, 1), 0)
    for half in range(2):
        pick = jnp.where(line == 2 * row + half, 1.0, 0.0).astype(jnp.bfloat16)
        out_ref[:, half * LANES:(half + 1) * LANES] = jnp.dot(
            pick, arrived_ref[...], preferred_element_type=jnp.float32
        ).astype(jnp.bfloat16)


def refresh_kernel(got_ref, *refs):
    *term_refs, out_ref = refs
    slots, width = out_ref.shape
    _, sources, _ = got_ref.shape
    cap = slots // sources
    meta = got_ref[2 * cap].astype(jnp.float32)
    parts = []
    for k in range(cap):
        rows = slice(k * sources, (k + 1) * sources)
        mixed = sum(ref[rows, :].astype(jnp.float32) for ref in term_refs)
        own = jnp.concatenate([got_ref[k], got_ref[cap + k]], axis=1).astype(jnp.float32)
        parts.append(jnp.where(meta[:, k:k + 1] >= 0.0, own + mixed, 0.0).astype(jnp.bfloat16))
    updated = jnp.concatenate(parts, axis=0)
    line = iota((1, slots), 1)
    row = iota((slots, 1), 0)
    pick = jnp.where((line & (sources - 1)) * cap + line // sources == row, 1.0, 0.0).astype(jnp.bfloat16)
    out_ref[...] = jnp.dot(pick, updated, preferred_element_type=jnp.float32).astype(jnp.bfloat16)


def call(kernel, out, args, scratch=(), smem=(), hbm=(), cost=None, vmem=VMEM):
    specs = [
        pl.BlockSpec(memory_space=pltpu.SMEM if i in smem else pltpu.HBM if i in hbm else pltpu.VMEM)
        for i in range(len(args))
    ]
    return pl.pallas_call(
        kernel,
        out_shape=out,
        in_specs=specs,
        out_specs=jax.tree.map(lambda _: pl.BlockSpec(memory_space=pltpu.VMEM), out),
        scratch_shapes=list(scratch),
        cost_estimate=cost,
        compiler_params=pltpu.CompilerParams(vmem_limit_bytes=vmem),
    )(*args)


def local(
    events, event_owner, event_user, cache_keys, cache_values, cache_len, user_rank,
    norm_gain, w_query, w_key, w_value, w_out,
):
    count, width = events.shape
    owners = lax.axis_size("users")
    groups = lax.axis_size("heads")
    cap = 2 * count // owners
    slots = owners * cap
    bf16 = jnp.bfloat16
    sent = call(
        functools.partial(route_kernel, owners, cap),
        jax.ShapeDtypeStruct((owners * CHUNK, LANES), bf16),
        (event_owner.reshape(1, count), event_user.reshape(1, count), events),
        scratch=[
            pltpu.VMEM((1, count), jnp.int32),
            pltpu.VMEM((1, count), jnp.int32),
            pltpu.VMEM((count, width), bf16),
            pltpu.SemaphoreType.DMA((3,)),
        ],
        hbm=(0, 1, 2),
        vmem=60 * 1024 * 1024,
    )
    got = lax.all_to_all(
        sent.reshape(owners, CHUNK // 2, 2, LANES), "users", split_axis=0, concat_axis=0, tiled=True
    )
    got = got.reshape(owners, CHUNK, LANES).transpose(1, 0, 2)
    own = got[:2 * cap]
    full = lax.all_to_all(
        jnp.broadcast_to(own, (groups,) + own.shape), "heads", split_axis=0, concat_axis=0, tiled=True
    )
    got, full = lax.optimization_barrier((got, full))
    own = got[:2 * cap]
    *terms, edge, base = call(
        attend_kernel,
        (jax.ShapeDtypeStruct((slots, width), bf16),) * groups
        + (
            jax.ShapeDtypeStruct((groups, EDGE, width), bf16),
            jax.ShapeDtypeStruct((EDGE, width), jnp.float32),
        ),
        (
            full, got, cache_len, norm_gain.reshape(1, -1), w_query, w_key, w_value,
            cache_keys[0], cache_values[0], w_out,
        ),
        scratch=[
            pltpu.VMEM((slots, groups * width), bf16),
            pltpu.VMEM((slots, width), bf16),
            pltpu.VMEM((slots, width), bf16),
            pltpu.VMEM((slots, width), bf16),
            pltpu.VMEM((slots, width), bf16),
        ],
        smem=(2,),
    )
    edge = lax.all_to_all(edge, "heads", split_axis=0, concat_axis=0, tiled=True)
    outgoing = call(
        functools.partial(state_kernel, owners),
        jax.ShapeDtypeStruct((owners * 4, LANES), bf16),
        (user_rank, base, edge),
        smem=(0,),
    )
    outgoing, terms = lax.optimization_barrier((outgoing, terms))
    terms = [terms[0]] + [
        lax.ppermute(terms[shift], "heads", [(g, (g + shift) % groups) for g in range(groups)])
        for shift in range(1, groups)
    ]
    arrived = lax.all_to_all(
        outgoing.reshape(owners, 4, LANES), "users", split_axis=0, concat_axis=0, tiled=True
    )
    ranked = call(
        ranked_kernel,
        jax.ShapeDtypeStruct((owners * 2, width), bf16),
        (arrived.reshape(owners * 4, LANES),),
        cost=pl.CostEstimate(flops=LAST_FLOPS, bytes_accessed=1 << 20, transcendentals=0),
    )
    refreshed = call(
        refresh_kernel,
        jax.ShapeDtypeStruct((slots, width), bf16),
        (got, *terms),
        cost=pl.CostEstimate(flops=300_000_000, bytes_accessed=1 << 20, transcendentals=0),
    )
    return refreshed[None], ranked[None]


def solution(mesh):
    placed = (
        P("users", "heads"),
        P("users", None),
        P("users"),
        P("users", None, None, "heads"),
        P("users", None, None, "heads"),
        P("users", None),
        P("users", None),
        P(),
        P(None, "heads"),
        P(None, "heads"),
        P(None, "heads"),
        P("heads", None),
    )
    return jax.shard_map(
        local,
        mesh=mesh,
        in_specs=placed,
        out_specs=(P("users", None, "heads"), P("users", None, "heads")),
        check_vma=False,
    )
```

time: 112 us -> 101 us (0.902)
  waiting for transfers between devices: 38.7 us -> 8.82 us
  blocking collectives: 34.8 us -> 60.2 us
  local copies, waits for them, and re-layouts: 9.25 us -> 1.63 us
    all_to_all x2 -> x0, waiting for transfers between devices: 27.3 us -> none  [the longest x1 13.9 us: local(): lax.all_to_all(jnp.broadcast_to(own, (groups,) + own.shape), 'heads', spl...]
    all_to_all x0 -> x2, blocking collectives: none -> 25.2 us  [the longest x1 18.6 us: local(): lax.all_to_all(jnp.broadcast_to(own, (groups,) + own.shape), 'heads', spl...]
    ppermute x0 -> x3, starting transfers between devices: none -> 8.6 us  [local(): lax.ppermute(terms[shift], 'heads', [(g, (g + shift) % groups) for g in r...]
    all_to_all x2 -> x0, starting transfers between devices: 7.81 us -> none  [the longest x1 4.16 us: local(): lax.all_to_all(jnp.broadcast_to(own, (groups,) + own.shape), 'heads', spl...]
    all_to_all x1, waiting for transfers between devices: 11.5 us -> 4.22 us  [local(): lax.all_to_all(outgoing.reshape(owners, 4, LANES), 'users', split_axis=0,...]
    ppermute x0 -> x3, waiting for transfers between devices: none -> 4.6 us  [local(): lax.ppermute(terms[shift], 'heads', [(g, (g + shift) % groups) for g in r...]
    unnamed x26 -> x18, local copies, waits for them, and re-layouts: 5.1 us -> 1.33 us
    reshape x3 -> x0, local copies, waits for them, and re-layouts: 1.7 us -> none  [the longest x1 0.77 us: local(): refreshed = updated.transpose(1, 0, 2).reshape(1, slots, width)]
  transfers between devices with their start and end apart: 3 -> 4, of which waited for: 3 -> 3; matrix products, arithmetic and copies ran while one was open for 2% -> 0% of each run, Pallas kernels for 0% -> 1%
where the time goes in v2:
time: 101 us; the launch traced here: 100 us
  blocking collectives  60.2 us (60%)
  starting transfers between devices  16.3 us (16%)
  Pallas kernels  12.2 us (12%)
  waiting for transfers between devices  8.82 us (9%)
  local copies, waits for them, and re-layouts  1.63 us (2%)
    all_to_all x1, blocking collectives, local(): lax.all_to_all(sent.reshape(owners, CHUNK // 2, 2, LANES), 'users', split...  35 us
    all_to_all x1, blocking collectives, local(): lax.all_to_all(jnp.broadcast_to(own, (groups,) + own.shape), 'heads', spl...  18.6 us
    pallas_call x5, Pallas kernels, call(): pl.pallas_call(kernel, out_shape=out, in_specs=specs, out_specs=jax.tree....  12.2 us
    ppermute x3, starting transfers between devices, local(): lax.ppermute(terms[shift], 'heads', [(g, (g + shift) % groups) for g in r...  8.6 us
    all_to_all x1, starting transfers between devices, local(): lax.all_to_all(outgoing.reshape(owners, 4, LANES), 'users', split_axis=0,...  7.75 us
    all_to_all x1, blocking collectives, local(): lax.all_to_all(edge, 'heads', split_axis=0, concat_axis=0, tiled=True)  6.65 us
    ppermute x3, waiting for transfers between devices, local(): lax.ppermute(terms[shift], 'heads', [(g, (g + shift) % groups) for g in r...  4.6 us
    all_to_all x1, waiting for transfers between devices, local(): lax.all_to_all(outgoing.reshape(owners, 4, LANES), 'users', split_axis=0,...  4.22 us
  transfers between devices with their start and end apart: 4, of which 3 were waited for; matrix products, arithmetic and copies ran while one was open for 0% of the time, Pallas kernels for 1%

profile of v2, /device:TPU:1, one launch (start us, length us, event | category | flops | bytes accessed | tf_op | source)
XLA Modules:
  0.0 100.0 jit_solution(11819754620095199096)
XLA Ops:
  0.6 2.8 %shard_map.131 = bf16[1280,128]{1,0:T(8,128)(2,1)} custom-call(s32[1,256]{1,0:T(1,128)} %bitcast.22, s32[1,256]{1,0:T(1,128)} %bitcast.23, bf16[256,256]{1,0:T(8,128)(2,1)} %events_hbm.1), custom_call_target="tpu_custom_call" | custom-call | tf_op jit(solution)/shard_map/pallas_call | solution.py:220
  3.4 35.0 %all_to_all.20 = bf16[128,5,2,128]{3,2,1,0:T(2,128)(2,1)S(1)} all-to-all(bf16[128,5,2,128]{3,2,1,0:T(2,128)(2,1)} %bitcast.20), channel_id=1, replica_groups=mesh['users'=128,'heads'=4] {'users'}, dimensions={0} | all-to-all | bytes 655360 | tf_op jit(solution)/shard_map/all_to_all | solution.py:254
  38.5 0.0 copy-start.4
  38.5 0.0 copy-start.5
  38.6 0.2 broadcast_in_dim.9
  38.8 0.0 copy-start
  38.8 0.0 copy-start.1
  38.8 0.0 copy-start.2
  38.8 0.0 copy-start.3
  38.8 18.6 %all_to_all.21.rows_ref = bf16[4,8,128,128]{3,2,1,0:T(8,128)(2,1)S(1)} all-to-all(bf16[4,8,128,128]{3,2,1,0:T(8,128)(2,1)S(1)} %broadcast_in_dim.9), channel_id=1, replica_groups=mesh['users'=128,'heads'=4] {'heads'}, dimensions={0} | all-to-all | bytes 2097152 | tf_op jit(solution)/shard_map/all_to_all | solution.py:259
  57.4 0.0 copy-done.4
  57.4 0.0 copy-done.5
  57.4 0.0 copy-done
  57.4 0.0 copy-done.1
  57.4 0.0 copy-done.2
  57.4 0.0 copy-done.3
  57.5 0.6 copy-done.6
  58.1 0.0 copy-done.8
  58.1 5.9 %shard_map.132 = (bf16[512,256]{1,0:T(8,128)(2,1)S(1)}, bf16[512,256]{1,0:T(8,128)(2,1)S(1)}, bf16[512,256]{1,0:T(8,128)(2,1)S(1)}, bf16[512,256]{1,0:T(8,128)(2...) custom-call(bf16[4,8,128,128]{3,2,1,0:T(8,128)(2,1)S(1)} %all_to_all.21.rows_ref, ...), custom_call_target="tpu_custom_call" | custom-call | tf_op jit(solution)/shard_map/pallas_call | solution.py:220
  64.0 6.7 %all_to_all.22.terms_ref = bf16[4,16,256]{2,1,0:T(8,128)(2,1)S(1)} all-to-all(bf16[4,16,256]{2,1,0:T(8,128)(2,1)S(1)} %get-tuple-element.18), channel_id=1, replica_groups=mesh['users'=128,'heads'=4] {'heads'}, dimensions={0} | all-to-all | bytes 65536 | tf_op jit(solution)/shard_map/all_to_all | solution.py:284
  70.6 0.7 copy-done.7
  71.3 1.4 %shard_map.133 = bf16[512,128]{1,0:T(8,128)(2,1)} custom-call(s32[1,2]{1,0:T(1,128)S(1)} %copy-done.7, f32[16,256]{1,0:T(8,128)S(1)} %get-tuple-element.17.base_ref, bf16[4,16,256]{2,1,0:T(8,128)(2,1)S(1)} %all_to_all.22.terms_ref), custom_call_target="tpu_custom_call" | custom-call | tf_op jit(solution)/shard_map/pallas_call | solution.py:220
  72.7 7.7 %all-to-all-start.3 = ((bf16[128,4,128]{2,1,0:T(4,128)(2,1)}), bf16[128,4,128]{2,1,0:T(4,128)(2,1)S(1)}, u32[]{:S(2)}, u32[]{:S(2)}) async-start(bf16[128,4,128]{2,1,0:T(4,128)(2,1)} %bitcast.10), calls=%async_computation.3 | async-start | bytes 262144 | tf_op jit(solution)/shard_map/all_to_all | solution.py:296
  80.5 2.2 %collective-permute-start = (bf16[512,256]{1,0:T(8,128)(2,1)S(1)}, bf16[512,256]{1,0:T(8,128)(2,1)S(1)}, u32[]{:S(2)}, u32[]{:S(2)}) collective-permute-start(bf16[512,256]{1,0:T(8,128)(2,1)S(1)} %get-tuple-element.24), channel_id=1, source_target_pairs={{0,1},{1,2},{2,3},{3,0},{4,5},{5,6},{6,7},{7,4},{8,9},{9,10},{10,1... | collective-permute-start | bytes 786440 | tf_op jit(solution)/shard_map/ppermute | solution.py:293
  82.7 3.7 %collective-permute-start.1 = (bf16[512,256]{1,0:T(8,128)(2,1)S(1)}, bf16[512,256]{1,0:T(8,128)(2,1)S(1)}, u32[]{:S(2)}, u32[]{:S(2)}) collective-permute-start(bf16[512,256]{1,0:T(8,128)(2,1)S(1)} %get-tuple-element.25), channel_id=1, source_target_pairs={{0,2},{1,3},{2,0},{3,1},{4,6},{5,7},{6,4},{7,5},{8,10},{9,11},{10,... | collective-permute-start | bytes 786440 | tf_op jit(solution)/shard_map/ppermute | solution.py:293
  86.4 2.7 %collective-permute-start.2 = (bf16[512,256]{1,0:T(8,128)(2,1)S(1)}, bf16[512,256]{1,0:T(8,128)(2,1)S(1)}, u32[]{:S(2)}, u32[]{:S(2)}) collective-permute-start(bf16[512,256]{1,0:T(8,128)(2,1)S(1)} %get-tuple-element.26), channel_id=1, source_target_pairs={{0,3},{1,0},{2,1},{3,2},{4,7},{5,4},{6,5},{7,6},{8,11},{9,8},{10,9... | collective-permute-start | bytes 786440 | tf_op jit(solution)/shard_map/ppermute | solution.py:293
  89.1 4.2 %all-to-all-done.3 = bf16[128,4,128]{2,1,0:T(4,128)(2,1)S(1)} async-done(((bf16[128,4,128]{2,1,0:T(4,128)(2,1)}), bf16[128,4,128]{2,1,0:T(4,128)(2,1)S(1)}, u32[]{:S(2)}, u32[]{:S(2)}) %all-to-all-start.3) | async-done | bytes 131104 | tf_op jit(solution)/shard_map/all_to_all | solution.py:296
  93.3 1.0 shard_map.135
  94.3 0.0 collective-permute-done.refs_1_
  94.3 1.1 %collective-permute-done.1.refs_2_ = bf16[512,256]{1,0:T(8,128)(2,1)S(1)} collective-permute-done((bf16[512,256]{1,0:T(8,128)(2,1)S(1)}, bf16[512,256]{1,0:T(8,128)(2,1)S(1)}, u32[]{:S(2)}, u32[]{:S(2)}) %collective-permute-start.1) | collective-permute-done | bytes 262176 | tf_op jit(solution)/shard_map/ppermute | solution.py:293
  95.4 3.5 %collective-permute-done.2.refs_3_ = bf16[512,256]{1,0:T(8,128)(2,1)S(1)} collective-permute-done((bf16[512,256]{1,0:T(8,128)(2,1)S(1)}, bf16[512,256]{1,0:T(8,128)(2,1)S(1)}, u32[]{:S(2)}, u32[]{:S(2)}) %collective-permute-start.2) | collective-permute-done | bytes 262176 | tf_op jit(solution)/shard_map/ppermute | solution.py:293
  98.9 1.2 %shard_map.134 = bf16[512,256]{1,0:T(8,128)(2,1)} custom-call(bf16[10,128,128]{2,1,0:T(8,128)(2,1)S(1)} %bitcast.15, bf16[512,256]{1,0:T(8,128)(2,1)S(1)} %get-tuple-element.23.refs_0_, bf16[512,256]{1,0:T(8,128)(2,1)S(1)} %collective-permute-done.refs_1_, bf16[512,256]{1,0:T(8,128)(2,1)S(1)} %collective-permute-done.1.refs_2_, ...), custom_call_target="tpu_custom_call" | custom-call | flops 300000000 | bytes 1048576 | tf_op jit(solution)/shard_map/pallas_call | solution.py:220
  (5 shorter events, 0.1 us)
Async XLA Ops:
  38.5 18.9 %copy-start.4 = (bf16[1,2,512,256]{3,2,1,0:T(8,128)(2,1)S(1)}, bf16[1,2,512,256]{3,2,1,0:T(8,128)(2,1)}, u32[]{:S(2)}) copy-start(bf16[1,2,512,256]{3,2,1,0:T(8,128)(2,1)} %param.16) | copy-start | bytes 1572868
  38.5 18.9 %copy-start.5 = (bf16[256,1024]{1,0:T(8,128)(2,1)S(1)}, bf16[256,1024]{1,0:T(8,128)(2,1)}, u32[]{:S(2)}) copy-start(bf16[256,1024]{1,0:T(8,128)(2,1)} %wo_ref.1) | copy-start | bytes 1572868
  38.8 18.6 %copy-start = (bf16[1024,256]{1,0:T(8,128)(2,1)S(1)}, bf16[1024,256]{1,0:T(8,128)(2,1)}, u32[]{:S(2)}) copy-start(bf16[1024,256]{1,0:T(8,128)(2,1)} %wq_ref.1) | copy-start | bytes 1572868
  38.8 18.6 %copy-start.1 = (bf16[1024,256]{1,0:T(8,128)(2,1)S(1)}, bf16[1024,256]{1,0:T(8,128)(2,1)}, u32[]{:S(2)}) copy-start(bf16[1024,256]{1,0:T(8,128)(2,1)} %wk_ref.1) | copy-start | bytes 1572868
  38.8 18.6 %copy-start.2 = (bf16[1024,256]{1,0:T(8,128)(2,1)S(1)}, bf16[1024,256]{1,0:T(8,128)(2,1)}, u32[]{:S(2)}) copy-start(bf16[1024,256]{1,0:T(8,128)(2,1)} %wv_ref.1) | copy-start | bytes 1572868
  38.8 18.6 %copy-start.3 = (bf16[1,2,512,256]{3,2,1,0:T(8,128)(2,1)S(1)}, bf16[1,2,512,256]{3,2,1,0:T(8,128)(2,1)}, u32[]{:S(2)}) copy-start(bf16[1,2,512,256]{3,2,1,0:T(8,128)(2,1)} %param.15) | copy-start | bytes 1572868
  57.4 0.7 copy-start.6
  57.4 0.7 copy-start.8
  70.6 0.7 copy-start.7
  72.7 20.6 %all-to-all-start.3 = ((bf16[128,4,128]{2,1,0:T(4,128)(2,1)}), bf16[128,4,128]{2,1,0:T(4,128)(2,1)S(1)}, u32[]{:S(2)}, u32[]{:S(2)}) async-start(bf16[128,4,128]{2,1,0:T(4,128)(2,1)} %bitcast.10), calls=%async_computation.3 | async-start | bytes 262144 | tf_op jit(solution)/shard_map/all_to_all | solution.py:296
  80.5 13.8 %collective-permute-start = (bf16[512,256]{1,0:T(8,128)(2,1)S(1)}, bf16[512,256]{1,0:T(8,128)(2,1)S(1)}, u32[]{:S(2)}, u32[]{:S(2)}) collective-permute-start(bf16[512,256]{1,0:T(8,128)(2,1)S(1)} %get-tuple-element.24), channel_id=1, source_target_pairs={{0,1},{1,2},{2,3},{3,0},{4,5},{5,6},{6,7},{7,4},{8,9},{9,10},{10,1... | collective-permute-start | bytes 786440 | tf_op jit(solution)/shard_map/ppermute | solution.py:293
  82.7 12.8 %collective-permute-start.1 = (bf16[512,256]{1,0:T(8,128)(2,1)S(1)}, bf16[512,256]{1,0:T(8,128)(2,1)S(1)}, u32[]{:S(2)}, u32[]{:S(2)}) collective-permute-start(bf16[512,256]{1,0:T(8,128)(2,1)S(1)} %get-tuple-element.25), channel_id=1, source_target_pairs={{0,2},{1,3},{2,0},{3,1},{4,6},{5,7},{6,4},{7,5},{8,10},{9,11},{10,... | collective-permute-start | bytes 786440 | tf_op jit(solution)/shard_map/ppermute | solution.py:293
  86.4 12.5 %collective-permute-start.2 = (bf16[512,256]{1,0:T(8,128)(2,1)S(1)}, bf16[512,256]{1,0:T(8,128)(2,1)S(1)}, u32[]{:S(2)}, u32[]{:S(2)}) collective-permute-start(bf16[512,256]{1,0:T(8,128)(2,1)S(1)} %get-tuple-element.26), channel_id=1, source_target_pairs={{0,3},{1,0},{2,1},{3,2},{4,7},{5,4},{6,5},{7,6},{8,11},{9,8},{10,9... | collective-permute-start | bytes 786440 | tf_op jit(solution)/shard_map/ppermute | solution.py:293

commit v3 on v2

--- a/solution.py
+++ b/solution.py
@@ -11,7 +11,7 @@
 LANES = 128
 CHUNK = 10
 BIG = 1e30
-LAST_FLOPS = 30_000_000_000
+PICK_FLOPS = 30_000_000_000
 STEP = 2
 EDGE = 16
 VMEM = 16 * 1024 * 1024
@@ -21,11 +21,17 @@
     return lax.broadcasted_iota(jnp.int32, shape, axis)
 
 
-def route_kernel(owners, cap, owner_hbm, user_hbm, events_hbm, out_ref, owner_ref, user_ref, events_ref, sems):
+def route_kernel(
+    owners, cap, owner_hbm, user_hbm, events_hbm, gain_hbm, len_hbm, rank_hbm,
+    out_ref, aux_ref, owner_ref, user_ref, events_ref, gain_ref, len_ref, rank_ref, sems,
+):
     copies = [
         pltpu.make_async_copy(source, target, sems.at[i])
         for i, (source, target) in enumerate(
-            [(owner_hbm, owner_ref), (user_hbm, user_ref), (events_hbm, events_ref)]
+            [
+                (owner_hbm, owner_ref), (user_hbm, user_ref), (events_hbm, events_ref),
+                (gain_hbm, gain_ref), (len_hbm, len_ref), (rank_hbm, rank_ref),
+            ]
         )
     ]
     for copy in copies:
@@ -54,13 +60,23 @@
     value = jnp.where(part < cap, rows[:, :LANES], rows[:, LANES:])
     value = jnp.where(part < 2 * cap, value, jnp.where(part == 2 * cap, users, 0.0))
     out_ref[...] = value.astype(jnp.bfloat16)
+    for copy in copies[3:]:
+        copy.wait()
+    wide = gain_ref.shape[1]
+    lane = iota((1, LANES), 1)
+    tail = jnp.where(lane == 0, len_ref[:, 0:1], jnp.where(lane == 1, len_ref[:, 1:2], 0))
+    tail = jnp.where(lane == 2, rank_ref[:, 0:1], jnp.where(lane == 3, rank_ref[:, 1:2], tail))
+    aux_ref[:, :wide] = gain_ref[...]
+    aux_ref[:, wide:] = tail.astype(jnp.float32)
 
 
 def attend_kernel(
-    rows_ref, got_ref, len_ref, gain_ref, wq_ref, wk_ref, wv_ref, ck_ref, cv_ref, wo_ref,
+    rows_ref, got_ref, aux_ref, wq_ref, wk_ref, wv_ref, ck_ref, cv_ref, wo_ref,
     own_ref, next_ref, across_ref, prev_ref, edge_ref, base_ref, normed_ref, query_ref, key_ref, value_ref, attn_ref,
 ):
     groups, parts, sources, _ = rows_ref.shape
+    width = own_ref.shape[1]
+    tail = aux_ref[:, groups * width:]
     cap = parts // 2
     slots = cap * sources
     depth = ck_ref.shape[1]
@@ -69,7 +85,7 @@
             [rows_ref[g, half * cap + k] for g in range(groups) for half in range(2)], axis=1
         ).astype(jnp.float32)
         mean = jnp.mean(wide * wide, axis=1, keepdims=True)
-        normed = wide * lax.rsqrt(mean + 1e-05) * gain_ref[...]
+        normed = wide * lax.rsqrt(mean + 1e-05) * aux_ref[:, :groups * width]
         normed_ref[k * sources:(k + 1) * sources, :] = normed.astype(jnp.bfloat16)
     normed = normed_ref[...]
     query = jnp.dot(normed, wq_ref[...], preferred_element_type=jnp.float32).astype(jnp.bfloat16)
@@ -85,11 +101,11 @@
     low_one = jnp.where(low, 1.0, 0.0).astype(jnp.bfloat16)
     high_one = jnp.where(low, 0.0, 1.0).astype(jnp.bfloat16)
     asks = jnp.where(lane == 0, 1.0 - second, jnp.where(lane == 1, second, 0.0)).astype(jnp.bfloat16)
-    place = iota((depth, 1), 0)
+    place = iota((depth, 1), 0).astype(jnp.float32)
     wrong_old = jnp.where(
         lane == 0,
-        jnp.where(place < len_ref[0, 0], 0.0, -BIG),
-        jnp.where(lane == 1, jnp.where(place < len_ref[0, 1], 0.0, -BIG), 0.0),
+        jnp.where(place < tail[:, 0:1], 0.0, -BIG),
+        jnp.where(lane == 1, jnp.where(place < tail[:, 1:2], 0.0, -BIG), 0.0),
     )
     wrong_new = jnp.where(
         lane == 0,
@@ -102,7 +118,7 @@
     col = iota((sources, sources), 1)
     upto = jnp.where(col <= row, 0.0, -BIG)
     under = jnp.where(col < row, 0.0, -BIG)
-    for pair in range(2):
+    def operands(pair):
         at = slice(pair * LANES, (pair + 1) * LANES)
         q, k_new, v_new = query_ref[:, at], key_ref[:, at], value_ref[:, at]
         k_one, v_one = ck_ref[0, :, at], cv_ref[0, :, at]
@@ -110,38 +126,53 @@
         k_two, v_two = pltpu.roll(ck_ref[1, :, at], HEAD_DIM, 1), pltpu.roll(cv_ref[1, :, at], HEAD_DIM, 1)
         for side in range(2):
             mine, other = (low_one, high_one) if side == 0 else (high_one, low_one)
-            in_mine, in_other = (low, ~low) if side == 0 else (~low, low)
+            in_mine = low if side == 0 else ~low
             held = jnp.where(in_mine, 1.0 - second, second).astype(jnp.bfloat16)
             queries = jnp.concatenate([(q * mine + q_turn * other) * held, asks], axis=1)
             keys = jnp.concatenate([k_one * mine + k_two * other, k_new * mine + k_turn * other], axis=0)
             keys = jnp.concatenate([keys, wrong], axis=1)
             values = jnp.concatenate([v_one * mine + v_two * other, v_new * mine + v_turn * other], axis=0)
             values = jnp.concatenate([values, ones], axis=1)
-            for t in range(0, cap, STEP):
-                rows = slice(t * sources, (t + STEP) * sources)
-                scores = lax.dot_general(
-                    queries[rows], keys, (((1,), (1,)), ((), ())), preferred_element_type=jnp.float32
-                )
-                bias = jnp.concatenate(
-                    [
-                        jnp.concatenate([upto if o <= k else under for o in range(cap)], axis=1)
-                        for k in range(t, t + STEP)
-                    ],
-                    axis=0,
-                )
-                old, fresh = scores[:, :depth], scores[:, depth:] + bias
-                top = jnp.maximum(jnp.max(old, axis=1, keepdims=True), jnp.max(fresh, axis=1, keepdims=True))
-                weights = jnp.concatenate(
-                    [jnp.exp(old - top).astype(jnp.bfloat16), jnp.exp(fresh - top).astype(jnp.bfloat16)], axis=1
-                )
-                mixed = jnp.dot(weights, values, preferred_element_type=jnp.float32)
-                mixed, total = mixed[:, :LANES], mixed[:, LANES:]
-                turned = pltpu.roll(mixed, HEAD_DIM, 1)
-                mixed = jnp.where(second[rows] == 1.0, turned, mixed) / total
-                here = slice(pair * LANES + side * HEAD_DIM, pair * LANES + (side + 1) * HEAD_DIM)
-                attn_ref[rows, here] = mixed[:, side * HEAD_DIM:(side + 1) * HEAD_DIM].astype(jnp.bfloat16)
+            yield queries, keys, values
+
+    heads = [head for pair in range(2) for head in operands(pair)]
+    steps = [(h, t) for h in range(len(heads)) for t in range(0, cap, STEP)]
+
+    def score(step):
+        h, t = step
+        queries, keys, _ = heads[h]
+        return lax.dot_general(
+            queries[t * sources:(t + STEP) * sources], keys, (((1,), (1,)), ((), ())),
+            preferred_element_type=jnp.float32,
+        )
+
+    ahead = score(steps[0])
+    for at, (h, t) in enumerate(steps):
+        scores = ahead
+        if at + 1 < len(steps):
+            ahead = score(steps[at + 1])
+        rows = slice(t * sources, (t + STEP) * sources)
+        bias = jnp.concatenate(
+            [
+                jnp.concatenate([upto if o <= k else under for o in range(cap)], axis=1)
+                for k in range(t, t + STEP)
+            ],
+            axis=0,
+        )
+        old, fresh = scores[:, :depth], scores[:, depth:] + bias
+        top = jnp.maximum(jnp.max(old, axis=1, keepdims=True), jnp.max(fresh, axis=1, keepdims=True))
+        weights = jnp.concatenate(
+            [jnp.exp(old - top).astype(jnp.bfloat16), jnp.exp(fresh - top).astype(jnp.bfloat16)], axis=1
+        )
+        mixed = jnp.dot(weights, heads[h][2], preferred_element_type=jnp.float32)
+        mixed, total = mixed[:, :LANES], mixed[:, LANES:]
+        turned = pltpu.roll(mixed, HEAD_DIM, 1)
+        mixed = jnp.where(second[rows] == 1.0, turned, mixed) / total
+        side = h % 2
+        attn_ref[rows, h * HEAD_DIM:(h + 1) * HEAD_DIM] = mixed[
+            :, side * HEAD_DIM:(side + 1) * HEAD_DIM
+        ].astype(jnp.bfloat16)
     attn = attn_ref[...]
-    width = own_ref.shape[1]
     source = iota((sources, 1), 0)
     lane_source = iota((1, sources), 1)
     which = iota((EDGE, 1), 0)
@@ -158,7 +189,9 @@
     for k in range(cap):
         own = jnp.concatenate([got_ref[k], got_ref[cap + k]], axis=1)
         base = base + jnp.dot(picks[k], own, preferred_element_type=jnp.float32)
-    base_ref[...] = base
+    base_ref[:EDGE] = base
+    base_ref[EDGE:, :LANES] = jnp.broadcast_to(tail, (8, LANES))
+    base_ref[EDGE:, LANES:] = jnp.zeros((8, width - LANES), jnp.float32)
     final = jnp.dot(jnp.concatenate(picks, axis=1), attn, preferred_element_type=jnp.float32).astype(jnp.bfloat16)
     me = lax.axis_index("heads")
     for shift, out_ref in enumerate((own_ref, next_ref, across_ref, prev_ref)):
@@ -168,8 +201,9 @@
         edge_ref[group] = jnp.dot(final, part, preferred_element_type=jnp.float32).astype(jnp.bfloat16)
 
 
-def state_kernel(owners, rank_ref, base_ref, terms_ref, out_ref):
-    state = base_ref[...]
+def state_kernel(owners, base_ref, terms_ref, out_ref):
+    state = base_ref[:EDGE]
+    ranks = base_ref[EDGE:EDGE + 1, :LANES].astype(jnp.int32)
     for g in range(terms_ref.shape[0]):
         state = state + terms_ref[g].astype(jnp.float32)
     line = iota((owners * 4, 1), 0)
@@ -177,7 +211,7 @@
     value = jnp.zeros((owners * 4, LANES), jnp.float32)
     for user in range(2):
         for half in range(2):
-            mine = (part == user * 2 + half) & (dest == rank_ref[0, user])
+            mine = (part == user * 2 + half) & (dest == ranks[:, 2 + user:3 + user])
             value = jnp.where(mine, state[user:user + 1, half * LANES:(half + 1) * LANES], value)
     out_ref[...] = value.astype(jnp.bfloat16)
 
@@ -238,17 +272,27 @@
     cap = 2 * count // owners
     slots = owners * cap
     bf16 = jnp.bfloat16
-    sent = call(
+    wide = groups * width
+    sent, aux = call(
         functools.partial(route_kernel, owners, cap),
-        jax.ShapeDtypeStruct((owners * CHUNK, LANES), bf16),
-        (event_owner.reshape(1, count), event_user.reshape(1, count), events),
+        (
+            jax.ShapeDtypeStruct((owners * CHUNK, LANES), bf16),
+            jax.ShapeDtypeStruct((1, wide + LANES), jnp.float32),
+        ),
+        (
+            event_owner.reshape(1, count), event_user.reshape(1, count), events,
+            norm_gain.reshape(1, wide), cache_len, user_rank,
+        ),
         scratch=[
             pltpu.VMEM((1, count), jnp.int32),
             pltpu.VMEM((1, count), jnp.int32),
             pltpu.VMEM((count, width), bf16),
-            pltpu.SemaphoreType.DMA((3,)),
+            pltpu.VMEM((1, wide), jnp.float32),
+            pltpu.VMEM((1, 2), jnp.int32),
+            pltpu.VMEM((1, 2), jnp.int32),
+            pltpu.SemaphoreType.DMA((6,)),
         ],
-        hbm=(0, 1, 2),
+        hbm=(0, 1, 2, 3, 4, 5),
         vmem=60 * 1024 * 1024,
     )
     got = lax.all_to_all(
@@ -266,10 +310,10 @@
         (jax.ShapeDtypeStruct((slots, width), bf16),) * groups
         + (
             jax.ShapeDtypeStruct((groups, EDGE, width), bf16),
-            jax.ShapeDtypeStruct((EDGE, width), jnp.float32),
+            jax.ShapeDtypeStruct((EDGE + 8, width), jnp.float32),
         ),
         (
-            full, got, cache_len, norm_gain.reshape(1, -1), w_query, w_key, w_value,
+            full, got, aux, w_query, w_key, w_value,
             cache_keys[0], cache_values[0], w_out,
         ),
         scratch=[
@@ -279,28 +323,30 @@
             pltpu.VMEM((slots, width), bf16),
             pltpu.VMEM((slots, width), bf16),
         ],
-        smem=(2,),
     )
     edge = lax.all_to_all(edge, "heads", split_axis=0, concat_axis=0, tiled=True)
     outgoing = call(
         functools.partial(state_kernel, owners),
         jax.ShapeDtypeStruct((owners * 4, LANES), bf16),
-        (user_rank, base, edge),
-        smem=(0,),
-    )
-    outgoing, terms = lax.optimization_barrier((outgoing, terms))
-    terms = [terms[0]] + [
-        lax.ppermute(terms[shift], "heads", [(g, (g + shift) % groups) for g in range(groups)])
-        for shift in range(1, groups)
-    ]
+        (base, edge),
+        cost=pl.CostEstimate(flops=PICK_FLOPS, bytes_accessed=1 << 20, transcendentals=0),
+    )
+    def passed(term, shift):
+        return lax.ppermute(term, "heads", [(g, (g + shift) % groups) for g in range(groups)])
+
+    across = passed(terms[2], 2)
+    outgoing, one, three = lax.optimization_barrier((outgoing, terms[1], terms[3]))
+    terms = [terms[0], passed(one, 1), across, passed(three, 3)]
     arrived = lax.all_to_all(
         outgoing.reshape(owners, 4, LANES), "users", split_axis=0, concat_axis=0, tiled=True
     )
+    arrived, across = lax.optimization_barrier((arrived, across))
+    terms[2] = across
     ranked = call(
         ranked_kernel,
         jax.ShapeDtypeStruct((owners * 2, width), bf16),
         (arrived.reshape(owners * 4, LANES),),
-        cost=pl.CostEstimate(flops=LAST_FLOPS, bytes_accessed=1 << 20, transcendentals=0),
+        cost=pl.CostEstimate(flops=PICK_FLOPS, bytes_accessed=1 << 20, transcendentals=0),
     )
     refreshed = call(
         refresh_kernel,

time: 101 us -> 95.7 us (0.948)
  blocking collectives: 60.2 us -> 53.6 us
  starting transfers between devices: 16.3 us -> 21.9 us
  waiting for transfers between devices: 8.82 us -> 6.33 us
    all_to_all x1 -> x0, blocking collectives: 6.65 us -> none  [local(): lax.all_to_all(edge, 'heads', split_axis=0, concat_axis=0, tiled=True)]
    ppermute x3, waiting for transfers between devices: 4.6 us -> 0.01 us  [passed(): lax.ppermute(term, 'heads', [(g, (g + shift) % groups) for g in range(gro...]
    all_to_all x0 -> x1, starting transfers between devices: none -> 3.26 us  [local(): lax.all_to_all(edge, 'heads', split_axis=0, concat_axis=0, tiled=True)]
    ppermute x3, starting transfers between devices: 8.6 us -> 11.3 us  [passed(): lax.ppermute(term, 'heads', [(g, (g + shift) % groups) for g in range(gro...]
    all_to_all x1, waiting for transfers between devices: 4.22 us -> 6.32 us  [local(): lax.all_to_all(outgoing.reshape(owners, 4, LANES), 'users', split_axis=0,...]
  transfers between devices with their start and end apart: 4 -> 5, of which waited for: 3 -> 1; matrix products, arithmetic and copies ran while one was open for 0% -> 0% of each run, Pallas kernels for 1% -> 2%
where the time goes in v3:
time: 95.7 us; the launch traced here: 95.2 us
  blocking collectives  53.6 us (56%)
  starting transfers between devices  21.9 us (23%)
  Pallas kernels  11.6 us (12%)
  waiting for transfers between devices  6.33 us (7%)
  local copies, waits for them, and re-layouts  0.98 us (1%)
    all_to_all x1, blocking collectives, local(): lax.all_to_all(sent.reshape(owners, CHUNK // 2, 2, LANES), 'users', split...  35 us
    all_to_all x1, blocking collectives, local(): lax.all_to_all(jnp.broadcast_to(own, (groups,) + own.shape), 'heads', spl...  18.6 us
    pallas_call x5, Pallas kernels, call(): pl.pallas_call(kernel, out_shape=out, in_specs=specs, out_specs=jax.tree....  11.6 us
    ppermute x3, starting transfers between devices, passed(): lax.ppermute(term, 'heads', [(g, (g + shift) % groups) for g in range(gro...  11.3 us
    all_to_all x1, starting transfers between devices, local(): lax.all_to_all(outgoing.reshape(owners, 4, LANES), 'users', split_axis=0,...  7.36 us
    all_to_all x1, waiting for transfers between devices, local(): lax.all_to_all(outgoing.reshape(owners, 4, LANES), 'users', split_axis=0,...  6.32 us
    all_to_all x1, starting transfers between devices, local(): lax.all_to_all(edge, 'heads', split_axis=0, concat_axis=0, tiled=True)  3.26 us
  transfers between devices with their start and end apart: 5, of which 1 were waited for; matrix products, arithmetic and copies ran while one was open for 0% of the time, Pallas kernels for 2%

profile of v3, /device:TPU:1, one launch (start us, length us, event | category | flops | bytes accessed | tf_op | source)
XLA Modules:
  0.0 95.2 jit_solution(6566871458167107766)
XLA Ops:
  0.6 2.8 %shard_map.131 = (bf16[1280,128]{1,0:T(8,128)(2,1)}, f32[1,1152]{1,0:T(1,128)}) custom-call(s32[1,256]{1,0:T(1,128)} %bitcast.22, s32[1,256]{1,0:T(1,128)} %bitcast.23, bf16[256,256]{1,0:T(8,128)(2,1)} %events_hbm.1, f32[1,1024]{1,0:T(1,128)} %bitcast.21, s32[1,2]{1,0:T(1,128)} %len_hbm.1, s32[1,2]{1,0:T(1,128)} %rank_hbm.1), custom_call_target="tpu_custom_call" | custom-call | tf_op jit(solution)/shard_map/pallas_call | solution.py:254
  3.5 35.0 %all_to_all.20 = bf16[128,5,2,128]{3,2,1,0:T(2,128)(2,1)S(1)} all-to-all(bf16[128,5,2,128]{3,2,1,0:T(2,128)(2,1)} %bitcast.19), channel_id=1, replica_groups=mesh['users'=128,'heads'=4] {'users'}, dimensions={0} | all-to-all | bytes 655360 | tf_op jit(solution)/shard_map/all_to_all | solution.py:298
  38.6 0.0 copy-start.4
  38.6 0.0 copy-start.5
  38.6 0.2 broadcast_in_dim.9
  38.8 0.0 copy-start
  38.8 0.0 copy-start.1
  38.8 0.0 copy-start.2
  38.9 0.0 copy-start.3
  38.9 18.6 %all_to_all.21.rows_ref = bf16[4,8,128,128]{3,2,1,0:T(8,128)(2,1)S(1)} all-to-all(bf16[4,8,128,128]{3,2,1,0:T(8,128)(2,1)S(1)} %broadcast_in_dim.9), channel_id=1, replica_groups=mesh['users'=128,'heads'=4] {'heads'}, dimensions={0} | all-to-all | bytes 2097152 | tf_op jit(solution)/shard_map/all_to_all | solution.py:303
  57.4 0.0 copy-start.6
  57.4 0.0 copy-done.4
  57.4 0.0 copy-done.5
  57.4 0.0 copy-done
  57.4 0.0 copy-done.1
  57.5 0.0 copy-done.2
  57.5 0.0 copy-done.3
  57.5 0.6 copy-done.6
  58.1 5.6 %shard_map.132 = (bf16[512,256]{1,0:T(8,128)(2,1)S(1)}, bf16[512,256]{1,0:T(8,128)(2,1)S(1)}, bf16[512,256]{1,0:T(8,128)(2,1)S(1)}, bf16[512,256]{1,0:T(8,128)(2...) custom-call(bf16[4,8,128,128]{3,2,1,0:T(8,128)(2,1)S(1)} %all_to_all.21.rows_ref, ...), custom_call_target="tpu_custom_call" | custom-call | tf_op jit(solution)/shard_map/pallas_call | solution.py:254
  63.8 3.3 %all-to-all-start.2 = ((bf16[4,16,256]{2,1,0:T(8,128)(2,1)}), bf16[4,16,256]{2,1,0:T(8,128)(2,1)S(1)}, u32[]{:S(2)}, u32[]{:S(2)}) async-start(bf16[4,16,256]{2,1,0:T(8,128)(2,1)} %get-tuple-element.23), calls=%async_computation.2 | async-start | bytes 65536 | tf_op jit(solution)/shard_map/all_to_all | solution.py:327
  67.0 4.8 %collective-permute-start.1 = (bf16[512,256]{1,0:T(8,128)(2,1)S(1)}, bf16[512,256]{1,0:T(8,128)(2,1)S(1)}, u32[]{:S(2)}, u32[]{:S(2)}) collective-permute-start(bf16[512,256]{1,0:T(8,128)(2,1)S(1)} %get-tuple-element.28), channel_id=1, source_target_pairs={{0,2},{1,3},{2,0},{3,1},{4,6},{5,7},{6,4},{7,5},{8,10},{9,11},{10,... | collective-permute-start | bytes 786440 | tf_op jit(solution)/shard_map/ppermute | solution.py:335
  71.9 0.0 all-to-all-done.2.terms_ref
  71.9 1.0 %shard_map.133 = bf16[512,128]{1,0:T(8,128)(2,1)} custom-call(f32[24,256]{1,0:T(8,128)S(1)} %get-tuple-element.22.base_ref, bf16[4,16,256]{2,1,0:T(8,128)(2,1)S(1)} %all-to-all-done.2.terms_ref), custom_call_target="tpu_custom_call" | custom-call | flops 30000001024 | bytes 1048576 | tf_op jit(solution)/shard_map/pallas_call | solution.py:254
  72.9 7.4 %all-to-all-start.3 = ((bf16[128,4,128]{2,1,0:T(4,128)(2,1)}), bf16[128,4,128]{2,1,0:T(4,128)(2,1)S(1)}, u32[]{:S(2)}, u32[]{:S(2)}) async-start(bf16[128,4,128]{2,1,0:T(4,128)(2,1)} %bitcast.9), calls=%async_computation.3 | async-start | bytes 262144 | tf_op jit(solution)/shard_map/all_to_all | solution.py:340
  80.3 2.0 %collective-permute-start = (bf16[512,256]{1,0:T(8,128)(2,1)S(1)}, bf16[512,256]{1,0:T(8,128)(2,1)S(1)}, u32[]{:S(2)}, u32[]{:S(2)}) collective-permute-start(bf16[512,256]{1,0:T(8,128)(2,1)S(1)} %get-tuple-element.26), channel_id=1, source_target_pairs={{0,1},{1,2},{2,3},{3,0},{4,5},{5,6},{6,7},{7,4},{8,9},{9,10},{10,1... | collective-permute-start | bytes 786440 | tf_op jit(solution)/shard_map/ppermute | solution.py:335
  82.3 4.5 %collective-permute-start.2 = (bf16[512,256]{1,0:T(8,128)(2,1)S(1)}, bf16[512,256]{1,0:T(8,128)(2,1)S(1)}, u32[]{:S(2)}, u32[]{:S(2)}) collective-permute-start(bf16[512,256]{1,0:T(8,128)(2,1)S(1)} %get-tuple-element.30), channel_id=1, source_target_pairs={{0,3},{1,0},{2,1},{3,2},{4,7},{5,4},{6,5},{7,6},{8,11},{9,8},{10,9... | collective-permute-start | bytes 786440 | tf_op jit(solution)/shard_map/ppermute | solution.py:335
  86.8 0.0 collective-permute-done.1.refs_2_
  86.8 6.3 %all-to-all-done.3 = bf16[128,4,128]{2,1,0:T(4,128)(2,1)S(1)} async-done(((bf16[128,4,128]{2,1,0:T(4,128)(2,1)}), bf16[128,4,128]{2,1,0:T(4,128)(2,1)S(1)}, u32[]{:S(2)}, u32[]{:S(2)}) %all-to-all-start.3) | async-done | bytes 131104 | tf_op jit(solution)/shard_map/all_to_all | solution.py:340
  93.1 1.0 %shard_map.135 = bf16[256,256]{1,0:T(8,128)(2,1)} custom-call(bf16[512,128]{1,0:T(8,128)(2,1)S(1)} %bitcast.18), custom_call_target="tpu_custom_call" | custom-call | flops 30000001024 | bytes 1048576 | tf_op jit(solution)/shard_map/pallas_call | solution.py:254
  94.1 0.0 collective-permute-done.refs_1_
  94.1 0.0 collective-permute-done.2.refs_3_
  94.1 1.2 %shard_map.134 = bf16[512,256]{1,0:T(8,128)(2,1)} custom-call(bf16[10,128,128]{2,1,0:T(8,128)(2,1)S(1)} %bitcast.15, bf16[512,256]{1,0:T(8,128)(2,1)S(1)} %get-tuple-element.21.refs_0_, bf16[512,256]{1,0:T(8,128)(2,1)S(1)} %collective-permute-done.refs_1_, bf16[512,256]{1,0:T(8,128)(2,1)S(1)} %collective-permute-done.1.refs_2_, ...), custom_call_target="tpu_custom_call" | custom-call | flops 300000000 | bytes 1048576 | tf_op jit(solution)/shard_map/pallas_call | solution.py:254
  (2 shorter events, 0.1 us)
Async XLA Ops:
  38.6 18.9 %copy-start.4 = (bf16[1,2,512,256]{3,2,1,0:T(8,128)(2,1)S(1)}, bf16[1,2,512,256]{3,2,1,0:T(8,128)(2,1)}, u32[]{:S(2)}) copy-start(bf16[1,2,512,256]{3,2,1,0:T(8,128)(2,1)} %param.16) | copy-start | bytes 1572868
  38.6 18.9 %copy-start.5 = (bf16[256,1024]{1,0:T(8,128)(2,1)S(1)}, bf16[256,1024]{1,0:T(8,128)(2,1)}, u32[]{:S(2)}) copy-start(bf16[256,1024]{1,0:T(8,128)(2,1)} %wo_ref.1) | copy-start | bytes 1572868
  38.8 18.6 %copy-start = (bf16[1024,256]{1,0:T(8,128)(2,1)S(1)}, bf16[1024,256]{1,0:T(8,128)(2,1)}, u32[]{:S(2)}) copy-start(bf16[1024,256]{1,0:T(8,128)(2,1)} %wq_ref.1) | copy-start | bytes 1572868
  38.8 18.6 %copy-start.1 = (bf16[1024,256]{1,0:T(8,128)(2,1)S(1)}, bf16[1024,256]{1,0:T(8,128)(2,1)}, u32[]{:S(2)}) copy-start(bf16[1024,256]{1,0:T(8,128)(2,1)} %wk_ref.1) | copy-start | bytes 1572868
  38.8 18.6 %copy-start.2 = (bf16[1024,256]{1,0:T(8,128)(2,1)S(1)}, bf16[1024,256]{1,0:T(8,128)(2,1)}, u32[]{:S(2)}) copy-start(bf16[1024,256]{1,0:T(8,128)(2,1)} %wv_ref.1) | copy-start | bytes 1572868
  38.9 18.6 %copy-start.3 = (bf16[1,2,512,256]{3,2,1,0:T(8,128)(2,1)S(1)}, bf16[1,2,512,256]{3,2,1,0:T(8,128)(2,1)}, u32[]{:S(2)}) copy-start(bf16[1,2,512,256]{3,2,1,0:T(8,128)(2,1)} %param.15) | copy-start | bytes 1572868
  57.4 0.7 copy-start.6
  63.8 8.1 %all-to-all-start.2 = ((bf16[4,16,256]{2,1,0:T(8,128)(2,1)}), bf16[4,16,256]{2,1,0:T(8,128)(2,1)S(1)}, u32[]{:S(2)}, u32[]{:S(2)}) async-start(bf16[4,16,256]{2,1,0:T(8,128)(2,1)} %get-tuple-element.23), calls=%async_computation.2 | async-start | bytes 65536 | tf_op jit(solution)/shard_map/all_to_all | solution.py:327
  67.0 19.7 %collective-permute-start.1 = (bf16[512,256]{1,0:T(8,128)(2,1)S(1)}, bf16[512,256]{1,0:T(8,128)(2,1)S(1)}, u32[]{:S(2)}, u32[]{:S(2)}) collective-permute-start(bf16[512,256]{1,0:T(8,128)(2,1)S(1)} %get-tuple-element.28), channel_id=1, source_target_pairs={{0,2},{1,3},{2,0},{3,1},{4,6},{5,7},{6,4},{7,5},{8,10},{9,11},{10,... | collective-permute-start | bytes 786440 | tf_op jit(solution)/shard_map/ppermute | solution.py:335
  72.9 20.2 %all-to-all-start.3 = ((bf16[128,4,128]{2,1,0:T(4,128)(2,1)}), bf16[128,4,128]{2,1,0:T(4,128)(2,1)S(1)}, u32[]{:S(2)}, u32[]{:S(2)}) async-start(bf16[128,4,128]{2,1,0:T(4,128)(2,1)} %bitcast.9), calls=%async_computation.3 | async-start | bytes 262144 | tf_op jit(solution)/shard_map/all_to_all | solution.py:340
  80.3 13.8 %collective-permute-start = (bf16[512,256]{1,0:T(8,128)(2,1)S(1)}, bf16[512,256]{1,0:T(8,128)(2,1)S(1)}, u32[]{:S(2)}, u32[]{:S(2)}) collective-permute-start(bf16[512,256]{1,0:T(8,128)(2,1)S(1)} %get-tuple-element.26), channel_id=1, source_target_pairs={{0,1},{1,2},{2,3},{3,0},{4,5},{5,6},{6,7},{7,4},{8,9},{9,10},{10,1... | collective-permute-start | bytes 786440 | tf_op jit(solution)/shard_map/ppermute | solution.py:335
  82.3 11.8 %collective-permute-start.2 = (bf16[512,256]{1,0:T(8,128)(2,1)S(1)}, bf16[512,256]{1,0:T(8,128)(2,1)S(1)}, u32[]{:S(2)}, u32[]{:S(2)}) collective-permute-start(bf16[512,256]{1,0:T(8,128)(2,1)S(1)} %get-tuple-element.30), channel_id=1, source_target_pairs={{0,3},{1,0},{2,1},{3,2},{4,7},{5,4},{6,5},{7,6},{8,11},{9,8},{10,9... | collective-permute-start | bytes 786440 | tf_op jit(solution)/shard_map/ppermute | solution.py:335

commit v4 on v3

--- a/solution.py
+++ b/solution.py
@@ -13,6 +13,7 @@
 BIG = 1e30
 PICK_FLOPS = 30_000_000_000
 STEP = 2
+PIECES = 32
 EDGE = 16
 VMEM = 16 * 1024 * 1024
 
@@ -23,7 +24,7 @@
 
 def route_kernel(
     owners, cap, owner_hbm, user_hbm, events_hbm, gain_hbm, len_hbm, rank_hbm,
-    out_ref, aux_ref, owner_ref, user_ref, events_ref, gain_ref, len_ref, rank_ref, sems,
+    out_hbm, made_ref, owner_ref, user_ref, events_ref, gain_ref, len_ref, rank_ref, sems,
 ):
     copies = [
         pltpu.make_async_copy(source, target, sems.at[i])
@@ -36,6 +37,12 @@
     ]
     for copy in copies:
         copy.start()
+    line = iota((owners * CHUNK, 1), 0)
+    dest = jnp.floor((line.astype(jnp.float32) + 0.5) * (1.0 / CHUNK)).astype(jnp.int32)
+    part = line - dest * CHUNK
+    slot = jnp.where(part >= cap, part - cap, part)
+    slot_line = jnp.where(part < 2 * cap, dest * CHUNK + slot, -1)
+    user_line = jnp.where(part == 2 * cap, dest, -1)
     copies[0].wait()
     copies[1].wait()
     owner = owner_ref[...]
@@ -46,37 +53,62 @@
     earlier = iota((count, count), 0) < iota((count, count), 1)
     rank = jnp.sum(jnp.where(earlier, same, 0.0), axis=0, keepdims=True).astype(jnp.int32)
     target = owner * CHUNK + rank
-    line = iota((owners * CHUNK, 1), 0)
-    dest = jnp.floor((line.astype(jnp.float32) + 0.5) * (1.0 / CHUNK)).astype(jnp.int32)
-    part = line - dest * CHUNK
-    slot = jnp.where(part >= cap, part - cap, part)
-    slot_line = jnp.where(part < 2 * cap, dest * CHUNK + slot, -1)
-    user_line = jnp.where(part == 2 * cap, dest, -1)
-    pick = jnp.where((slot_line == target) | (user_line == owner), 1.0, 0.0).astype(jnp.bfloat16)
-    copies[2].wait()
-    rows = jnp.dot(pick, events_ref[...], preferred_element_type=jnp.float32)
     named = jnp.where(iota((LANES, count), 0) == rank, user + 1, 0).astype(jnp.float32).astype(jnp.bfloat16)
-    users = lax.dot_general(pick, named, (((1,), (1,)), ((), ())), preferred_element_type=jnp.float32) - 1.0
-    value = jnp.where(part < cap, rows[:, :LANES], rows[:, LANES:])
-    value = jnp.where(part < 2 * cap, value, jnp.where(part == 2 * cap, users, 0.0))
-    out_ref[...] = value.astype(jnp.bfloat16)
-    for copy in copies[3:]:
+    for copy in copies[2:]:
         copy.wait()
-    wide = gain_ref.shape[1]
+    me = lax.axis_index("users")
+    piece = lax.rem(me, PIECES)
+    gain = gain_ref[:, pl.ds(pl.multiple_of(lax.rem(piece, PIECES // 4) * LANES, LANES), LANES)]
+    coarse = gain.astype(jnp.bfloat16).astype(jnp.float32)
+    middle = (gain - coarse).astype(jnp.bfloat16).astype(jnp.float32)
+    level = piece // (PIECES // 4)
+    spare = jnp.where(level == 0, coarse, jnp.where(level == 1, middle, gain - coarse - middle))
+    spare = jnp.where(level == 3, 0.0, spare)
     lane = iota((1, LANES), 1)
-    tail = jnp.where(lane == 0, len_ref[:, 0:1], jnp.where(lane == 1, len_ref[:, 1:2], 0))
-    tail = jnp.where(lane == 2, rank_ref[:, 0:1], jnp.where(lane == 3, rank_ref[:, 1:2], tail))
-    aux_ref[:, :wide] = gain_ref[...]
-    aux_ref[:, wide:] = tail.astype(jnp.float32)
+    back = jnp.zeros((1, LANES), jnp.int32)
+    for user_at in range(2):
+        length = len_ref[:, user_at:user_at + 1]
+        back = jnp.where(lane == 3 * user_at, length >> 4, back)
+        back = jnp.where(lane == 3 * user_at + 1, length & 15, back)
+        back = jnp.where(lane == 3 * user_at + 2, rank_ref[:, user_at:user_at + 1], back)
+    back = back.astype(jnp.float32)
+    events = events_ref[...]
+    half_lines = owners * CHUNK // 2
+    leaving = []
+    for half in range(2):
+        at = slice(half * half_lines, (half + 1) * half_lines)
+        pick = jnp.where((slot_line[at] == target) | (user_line[at] == owner), 1.0, 0.0).astype(jnp.bfloat16)
+        rows = jnp.dot(pick, events, preferred_element_type=jnp.float32)
+        users = lax.dot_general(pick, named, (((1,), (1,)), ((), ())), preferred_element_type=jnp.float32) - 1.0
+        value = jnp.where(part[at] < cap, rows[:, :LANES], rows[:, LANES:])
+        value = jnp.where(part[at] < 2 * cap, value, users)
+        value = jnp.where(part[at] > 2 * cap, jnp.where(dest[at] == me, back, spare), value)
+        made_ref[at, :] = value.astype(jnp.bfloat16)
+        leaving.append(pltpu.make_async_copy(made_ref.at[at], out_hbm.at[at], sems.at[len(copies) + half]))
+        leaving[half].start()
+    for copy in leaving:
+        copy.wait()
 
 
 def attend_kernel(
-    rows_ref, got_ref, aux_ref, wq_ref, wk_ref, wv_ref, ck_ref, cv_ref, wo_ref,
-    own_ref, next_ref, across_ref, prev_ref, edge_ref, base_ref, normed_ref, query_ref, key_ref, value_ref, attn_ref,
+    rows_ref, got_ref, wq_ref, wk_ref, wv_ref, ck_ref, cv_ref, wo_ref,
+    own_ref, next_ref, across_ref, prev_ref, edge_hbm, base_ref, normed_ref, query_ref, key_ref, value_ref, attn_ref,
+    edge_ref, sem,
 ):
     groups, parts, sources, _ = rows_ref.shape
     width = own_ref.shape[1]
-    tail = aux_ref[:, groups * width:]
+    me_user = lax.axis_index("users")
+    block = me_user // PIECES
+    beside = jnp.where(block % 2 == 0, block + 1, block - 1)
+    spare = got_ref[parts + 1, pl.ds(pl.multiple_of(beside * PIECES, PIECES), PIECES), :].astype(jnp.float32)
+    fourth = PIECES // 4
+    gain = spare[:fourth] + spare[fourth:2 * fourth] + spare[2 * fourth:3 * fourth]
+    gain = jnp.concatenate([gain[g:g + 1] for g in range(fourth)], axis=1)
+    back = got_ref[parts + 1, pl.ds(pl.multiple_of(block * PIECES, PIECES), PIECES), :].astype(jnp.float32)
+    back = jnp.where(iota((PIECES, 1), 0) == lax.rem(me_user, PIECES), back, 0.0)
+    back = jnp.sum(back, axis=0, keepdims=True)
+    lengths = [back[:, 3 * user:3 * user + 1] * 16.0 + back[:, 3 * user + 1:3 * user + 2] for user in range(2)]
+    ranks = [back[:, 3 * user + 2:3 * user + 3] for user in range(2)]
     cap = parts // 2
     slots = cap * sources
     depth = ck_ref.shape[1]
@@ -85,7 +117,7 @@
             [rows_ref[g, half * cap + k] for g in range(groups) for half in range(2)], axis=1
         ).astype(jnp.float32)
         mean = jnp.mean(wide * wide, axis=1, keepdims=True)
-        normed = wide * lax.rsqrt(mean + 1e-05) * aux_ref[:, :groups * width]
+        normed = wide * lax.rsqrt(mean + 1e-05) * gain
         normed_ref[k * sources:(k + 1) * sources, :] = normed.astype(jnp.bfloat16)
     normed = normed_ref[...]
     query = jnp.dot(normed, wq_ref[...], preferred_element_type=jnp.float32).astype(jnp.bfloat16)
@@ -104,8 +136,8 @@
     place = iota((depth, 1), 0).astype(jnp.float32)
     wrong_old = jnp.where(
         lane == 0,
-        jnp.where(place < tail[:, 0:1], 0.0, -BIG),
-        jnp.where(lane == 1, jnp.where(place < tail[:, 1:2], 0.0, -BIG), 0.0),
+        jnp.where(place < lengths[0], 0.0, -BIG),
+        jnp.where(lane == 1, jnp.where(place < lengths[1], 0.0, -BIG), 0.0),
     )
     wrong_new = jnp.where(
         lane == 0,
@@ -190,15 +222,20 @@
         own = jnp.concatenate([got_ref[k], got_ref[cap + k]], axis=1)
         base = base + jnp.dot(picks[k], own, preferred_element_type=jnp.float32)
     base_ref[:EDGE] = base
-    base_ref[EDGE:, :LANES] = jnp.broadcast_to(tail, (8, LANES))
-    base_ref[EDGE:, LANES:] = jnp.zeros((8, width - LANES), jnp.float32)
+    spot = iota((8, width), 1)
+    base_ref[EDGE:] = jnp.where(spot == 2, ranks[0], jnp.where(spot == 3, ranks[1], 0.0))
     final = jnp.dot(jnp.concatenate(picks, axis=1), attn, preferred_element_type=jnp.float32).astype(jnp.bfloat16)
     me = lax.axis_index("heads")
+    for group in range(groups):
+        part = wo_ref[:, group * width:(group + 1) * width]
+        edge_ref[group] = jnp.dot(final, part, preferred_element_type=jnp.float32).astype(jnp.bfloat16)
+    leave = pltpu.make_async_copy(edge_ref, edge_hbm, sem)
+    leave.start()
     for shift, out_ref in enumerate((own_ref, next_ref, across_ref, prev_ref)):
         group = lax.rem(me + shift, groups)
         part = wo_ref[:, pl.ds(pl.multiple_of(group * width, width), width)]
         out_ref[...] = jnp.dot(attn, part, preferred_element_type=jnp.float32).astype(jnp.bfloat16)
-        edge_ref[group] = jnp.dot(final, part, preferred_element_type=jnp.float32).astype(jnp.bfloat16)
+    leave.wait()
 
 
 def state_kernel(owners, base_ref, terms_ref, out_ref):
@@ -246,7 +283,7 @@
     out_ref[...] = jnp.dot(pick, updated, preferred_element_type=jnp.float32).astype(jnp.bfloat16)
 
 
-def call(kernel, out, args, scratch=(), smem=(), hbm=(), cost=None, vmem=VMEM):
+def call(kernel, out, args, scratch=(), smem=(), hbm=(), out_hbm=None, cost=None, vmem=VMEM):
     specs = [
         pl.BlockSpec(memory_space=pltpu.SMEM if i in smem else pltpu.HBM if i in hbm else pltpu.VMEM)
         for i in range(len(args))
@@ -255,7 +292,9 @@
         kernel,
         out_shape=out,
         in_specs=specs,
-        out_specs=jax.tree.map(lambda _: pl.BlockSpec(memory_space=pltpu.VMEM), out),
+        out_specs=jax.tree.map(
+            lambda o: pl.BlockSpec(memory_space=pltpu.HBM if out_hbm == o.shape else pltpu.VMEM), out
+        ),
         scratch_shapes=list(scratch),
         cost_estimate=cost,
         compiler_params=pltpu.CompilerParams(vmem_limit_bytes=vmem),
@@ -273,26 +312,25 @@
     slots = owners * cap
     bf16 = jnp.bfloat16
     wide = groups * width
-    sent, aux = call(
+    sent = call(
         functools.partial(route_kernel, owners, cap),
-        (
-            jax.ShapeDtypeStruct((owners * CHUNK, LANES), bf16),
-            jax.ShapeDtypeStruct((1, wide + LANES), jnp.float32),
-        ),
+        jax.ShapeDtypeStruct((owners * CHUNK, LANES), bf16),
         (
             event_owner.reshape(1, count), event_user.reshape(1, count), events,
             norm_gain.reshape(1, wide), cache_len, user_rank,
         ),
         scratch=[
+            pltpu.VMEM((owners * CHUNK, LANES), bf16),
             pltpu.VMEM((1, count), jnp.int32),
             pltpu.VMEM((1, count), jnp.int32),
             pltpu.VMEM((count, width), bf16),
             pltpu.VMEM((1, wide), jnp.float32),
             pltpu.VMEM((1, 2), jnp.int32),
             pltpu.VMEM((1, 2), jnp.int32),
-            pltpu.SemaphoreType.DMA((6,)),
+            pltpu.SemaphoreType.DMA((8,)),
         ],
         hbm=(0, 1, 2, 3, 4, 5),
+        out_hbm=(owners * CHUNK, LANES),
         vmem=60 * 1024 * 1024,
     )
     got = lax.all_to_all(
@@ -313,7 +351,7 @@
             jax.ShapeDtypeStruct((EDGE + 8, width), jnp.float32),
         ),
         (
-            full, got, aux, w_query, w_key, w_value,
+            full, got, w_query, w_key, w_value,
             cache_keys[0], cache_values[0], w_out,
         ),
         scratch=[
@@ -322,7 +360,10 @@
             pltpu.VMEM((slots, width), bf16),
             pltpu.VMEM((slots, width), bf16),
             pltpu.VMEM((slots, width), bf16),
+            pltpu.VMEM((groups, EDGE, width), bf16),
+            pltpu.SemaphoreType.DMA,
         ],
+        out_hbm=(groups, EDGE, width),
     )
     edge = lax.all_to_all(edge, "heads", split_axis=0, concat_axis=0, tiled=True)
     outgoing = call(

time: 95.7 us -> 94 us (0.982)
  Pallas kernels: 11.6 us -> 10.5 us
    pallas_call x5, Pallas kernels: 11.6 us -> 10.5 us  [call(): pl.pallas_call(kernel, out_shape=out, in_specs=specs, out_specs=jax.tree....]
where the time goes in v4:
time: 94 us; the launch traced here: 93.5 us
  blocking collectives  53.6 us (57%)
  starting transfers between devices  22 us (23%)
  Pallas kernels  10.5 us (11%)
  waiting for transfers between devices  6.33 us (7%)
    all_to_all x1, blocking collectives, local(): lax.all_to_all(sent.reshape(owners, CHUNK // 2, 2, LANES), 'users', split...  35 us
    all_to_all x1, blocking collectives, local(): lax.all_to_all(jnp.broadcast_to(own, (groups,) + own.shape), 'heads', spl...  18.6 us
    ppermute x3, starting transfers between devices, passed(): lax.ppermute(term, 'heads', [(g, (g + shift) % groups) for g in range(gro...  11.3 us
    pallas_call x5, Pallas kernels, call(): pl.pallas_call(kernel, out_shape=out, in_specs=specs, out_specs=jax.tree....  10.5 us
    all_to_all x1, starting transfers between devices, local(): lax.all_to_all(outgoing.reshape(owners, 4, LANES), 'users', split_axis=0,...  7.36 us
    all_to_all x1, waiting for transfers between devices, local(): lax.all_to_all(outgoing.reshape(owners, 4, LANES), 'users', split_axis=0,...  6.32 us
    all_to_all x1, starting transfers between devices, local(): lax.all_to_all(edge, 'heads', split_axis=0, concat_axis=0, tiled=True)  3.28 us
  transfers between devices with their start and end apart: 5, of which 1 were waited for; matrix products, arithmetic and copies ran while one was open for 0% of the time, Pallas kernels for 2%

profile of v4, /device:TPU:1, one launch (start us, length us, event | category | flops | bytes accessed | tf_op | source)
XLA Modules:
  0.0 93.5 jit_solution(1084761751265848088)
XLA Ops:
  0.6 2.2 %shard_map.131 = bf16[1280,128]{1,0:T(8,128)(2,1)} custom-call(s32[1,256]{1,0:T(1,128)} %bitcast.22, s32[1,256]{1,0:T(1,128)} %bitcast.23, bf16[256,256]{1,0:T(8,128)(2,1)} %events_hbm.1, f32[1,1024]{1,0:T(1,128)} %bitcast.21, s32[1,2]{1,0:T(1,128)} %len_hbm.1, s32[1,2]{1,0:T(1,128)} %rank_hbm.1), custom_call_target="tpu_custom_call" | custom-call | tf_op jit(solution)/shard_map/pallas_call | solution.py:291
  2.8 35.0 %all_to_all.20 = bf16[128,5,2,128]{3,2,1,0:T(2,128)(2,1)S(1)} all-to-all(bf16[128,5,2,128]{3,2,1,0:T(2,128)(2,1)} %bitcast.19), channel_id=1, replica_groups=mesh['users'=128,'heads'=4] {'users'}, dimensions={0} | all-to-all | bytes 655360 | tf_op jit(solution)/shard_map/all_to_all | solution.py:336
  37.9 0.0 copy-start.4
  37.9 0.0 copy-start.5
  38.0 0.2 broadcast_in_dim.9
  38.2 0.0 copy-start
  38.2 0.0 copy-start.1
  38.2 0.0 copy-start.2
  38.2 0.0 copy-start.3
  38.2 18.6 %all_to_all.21.rows_ref = bf16[4,8,128,128]{3,2,1,0:T(8,128)(2,1)S(1)} all-to-all(bf16[4,8,128,128]{3,2,1,0:T(8,128)(2,1)S(1)} %broadcast_in_dim.9), channel_id=1, replica_groups=mesh['users'=128,'heads'=4] {'heads'}, dimensions={0} | all-to-all | bytes 2097152 | tf_op jit(solution)/shard_map/all_to_all | solution.py:341
  56.8 0.0 copy-done.4
  56.8 0.0 copy-done.5
  56.8 0.0 copy-done
  56.8 0.0 copy-done.1
  56.8 0.0 copy-done.2
  56.8 0.0 copy-done.3
  56.8 5.2 %shard_map.132 = (bf16[512,256]{1,0:T(8,128)(2,1)S(1)}, bf16[512,256]{1,0:T(8,128)(2,1)S(1)}, bf16[512,256]{1,0:T(8,128)(2,1)S(1)}, bf16[512,256]{1,0:T(8,128)(2...) custom-call(bf16[4,8,128,128]{3,2,1,0:T(8,128)(2,1)S(1)} %all_to_all.21.rows_ref, ...), custom_call_target="tpu_custom_call" | custom-call | tf_op jit(solution)/shard_map/pallas_call | solution.py:291
  62.0 3.3 %all-to-all-start.2 = ((bf16[4,16,256]{2,1,0:T(8,128)(2,1)}), bf16[4,16,256]{2,1,0:T(8,128)(2,1)S(1)}, u32[]{:S(2)}, u32[]{:S(2)}) async-start(bf16[4,16,256]{2,1,0:T(8,128)(2,1)} %get-tuple-element.19), calls=%async_computation.2 | async-start | bytes 65536 | tf_op jit(solution)/shard_map/all_to_all | solution.py:368
  65.3 4.8 %collective-permute-start.1 = (bf16[512,256]{1,0:T(8,128)(2,1)S(1)}, bf16[512,256]{1,0:T(8,128)(2,1)S(1)}, u32[]{:S(2)}, u32[]{:S(2)}) collective-permute-start(bf16[512,256]{1,0:T(8,128)(2,1)S(1)} %get-tuple-element.24), channel_id=1, source_target_pairs={{0,2},{1,3},{2,0},{3,1},{4,6},{5,7},{6,4},{7,5},{8,10},{9,11},{10,... | collective-permute-start | bytes 786440 | tf_op jit(solution)/shard_map/ppermute | solution.py:376
  70.2 0.0 all-to-all-done.2.terms_ref
  70.2 1.0 %shard_map.133 = bf16[512,128]{1,0:T(8,128)(2,1)} custom-call(f32[24,256]{1,0:T(8,128)S(1)} %get-tuple-element.18.base_ref, bf16[4,16,256]{2,1,0:T(8,128)(2,1)S(1)} %all-to-all-done.2.terms_ref), custom_call_target="tpu_custom_call" | custom-call | flops 30000001024 | bytes 1048576 | tf_op jit(solution)/shard_map/pallas_call | solution.py:291
  71.2 7.4 %all-to-all-start.3 = ((bf16[128,4,128]{2,1,0:T(4,128)(2,1)}), bf16[128,4,128]{2,1,0:T(4,128)(2,1)S(1)}, u32[]{:S(2)}, u32[]{:S(2)}) async-start(bf16[128,4,128]{2,1,0:T(4,128)(2,1)} %bitcast.9), calls=%async_computation.3 | async-start | bytes 262144 | tf_op jit(solution)/shard_map/all_to_all | solution.py:381
  78.5 2.0 %collective-permute-start = (bf16[512,256]{1,0:T(8,128)(2,1)S(1)}, bf16[512,256]{1,0:T(8,128)(2,1)S(1)}, u32[]{:S(2)}, u32[]{:S(2)}) collective-permute-start(bf16[512,256]{1,0:T(8,128)(2,1)S(1)} %get-tuple-element.22), channel_id=1, source_target_pairs={{0,1},{1,2},{2,3},{3,0},{4,5},{5,6},{6,7},{7,4},{8,9},{9,10},{10,1... | collective-permute-start | bytes 786440 | tf_op jit(solution)/shard_map/ppermute | solution.py:376
  80.5 4.5 %collective-permute-start.2 = (bf16[512,256]{1,0:T(8,128)(2,1)S(1)}, bf16[512,256]{1,0:T(8,128)(2,1)S(1)}, u32[]{:S(2)}, u32[]{:S(2)}) collective-permute-start(bf16[512,256]{1,0:T(8,128)(2,1)S(1)} %get-tuple-element.26), channel_id=1, source_target_pairs={{0,3},{1,0},{2,1},{3,2},{4,7},{5,4},{6,5},{7,6},{8,11},{9,8},{10,9... | collective-permute-start | bytes 786440 | tf_op jit(solution)/shard_map/ppermute | solution.py:376
  85.1 0.0 collective-permute-done.1.refs_2_
  85.1 6.3 %all-to-all-done.3 = bf16[128,4,128]{2,1,0:T(4,128)(2,1)S(1)} async-done(((bf16[128,4,128]{2,1,0:T(4,128)(2,1)}), bf16[128,4,128]{2,1,0:T(4,128)(2,1)S(1)}, u32[]{:S(2)}, u32[]{:S(2)}) %all-to-all-start.3) | async-done | bytes 131104 | tf_op jit(solution)/shard_map/all_to_all | solution.py:381
  91.4 1.0 %shard_map.135 = bf16[256,256]{1,0:T(8,128)(2,1)} custom-call(bf16[512,128]{1,0:T(8,128)(2,1)S(1)} %bitcast.18), custom_call_target="tpu_custom_call" | custom-call | flops 30000001024 | bytes 1048576 | tf_op jit(solution)/shard_map/pallas_call | solution.py:291
  92.4 0.0 collective-permute-done.refs_1_
  92.4 0.0 collective-permute-done.2.refs_3_
  92.4 1.2 %shard_map.134 = bf16[512,256]{1,0:T(8,128)(2,1)} custom-call(bf16[10,128,128]{2,1,0:T(8,128)(2,1)S(1)} %bitcast.15, bf16[512,256]{1,0:T(8,128)(2,1)S(1)} %get-tuple-element.17.refs_0_, bf16[512,256]{1,0:T(8,128)(2,1)S(1)} %collective-permute-done.refs_1_, bf16[512,256]{1,0:T(8,128)(2,1)S(1)} %collective-permute-done.1.refs_2_, ...), custom_call_target="tpu_custom_call" | custom-call | flops 300000000 | bytes 1048576 | tf_op jit(solution)/shard_map/pallas_call | solution.py:291
  (2 shorter events, 0.1 us)
Async XLA Ops:
  37.9 18.9 %copy-start.4 = (bf16[1,2,512,256]{3,2,1,0:T(8,128)(2,1)S(1)}, bf16[1,2,512,256]{3,2,1,0:T(8,128)(2,1)}, u32[]{:S(2)}) copy-start(bf16[1,2,512,256]{3,2,1,0:T(8,128)(2,1)} %param.16) | copy-start | bytes 1572868
  37.9 18.9 %copy-start.5 = (bf16[256,1024]{1,0:T(8,128)(2,1)S(1)}, bf16[256,1024]{1,0:T(8,128)(2,1)}, u32[]{:S(2)}) copy-start(bf16[256,1024]{1,0:T(8,128)(2,1)} %wo_ref.1) | copy-start | bytes 1572868
  38.2 18.6 %copy-start = (bf16[1024,256]{1,0:T(8,128)(2,1)S(1)}, bf16[1024,256]{1,0:T(8,128)(2,1)}, u32[]{:S(2)}) copy-start(bf16[1024,256]{1,0:T(8,128)(2,1)} %wq_ref.1) | copy-start | bytes 1572868
  38.2 18.6 %copy-start.1 = (bf16[1024,256]{1,0:T(8,128)(2,1)S(1)}, bf16[1024,256]{1,0:T(8,128)(2,1)}, u32[]{:S(2)}) copy-start(bf16[1024,256]{1,0:T(8,128)(2,1)} %wk_ref.1) | copy-start | bytes 1572868
  38.2 18.6 %copy-start.2 = (bf16[1024,256]{1,0:T(8,128)(2,1)S(1)}, bf16[1024,256]{1,0:T(8,128)(2,1)}, u32[]{:S(2)}) copy-start(bf16[1024,256]{1,0:T(8,128)(2,1)} %wv_ref.1) | copy-start | bytes 1572868
  38.2 18.6 %copy-start.3 = (bf16[1,2,512,256]{3,2,1,0:T(8,128)(2,1)S(1)}, bf16[1,2,512,256]{3,2,1,0:T(8,128)(2,1)}, u32[]{:S(2)}) copy-start(bf16[1,2,512,256]{3,2,1,0:T(8,128)(2,1)} %param.15) | copy-start | bytes 1572868
  62.0 8.1 %all-to-all-start.2 = ((bf16[4,16,256]{2,1,0:T(8,128)(2,1)}), bf16[4,16,256]{2,1,0:T(8,128)(2,1)S(1)}, u32[]{:S(2)}, u32[]{:S(2)}) async-start(bf16[4,16,256]{2,1,0:T(8,128)(2,1)} %get-tuple-element.19), calls=%async_computation.2 | async-start | bytes 65536 | tf_op jit(solution)/shard_map/all_to_all | solution.py:368
  65.3 19.7 %collective-permute-start.1 = (bf16[512,256]{1,0:T(8,128)(2,1)S(1)}, bf16[512,256]{1,0:T(8,128)(2,1)S(1)}, u32[]{:S(2)}, u32[]{:S(2)}) collective-permute-start(bf16[512,256]{1,0:T(8,128)(2,1)S(1)} %get-tuple-element.24), channel_id=1, source_target_pairs={{0,2},{1,3},{2,0},{3,1},{4,6},{5,7},{6,4},{7,5},{8,10},{9,11},{10,... | collective-permute-start | bytes 786440 | tf_op jit(solution)/shard_map/ppermute | solution.py:376
  71.2 20.2 %all-to-all-start.3 = ((bf16[128,4,128]{2,1,0:T(4,128)(2,1)}), bf16[128,4,128]{2,1,0:T(4,128)(2,1)S(1)}, u32[]{:S(2)}, u32[]{:S(2)}) async-start(bf16[128,4,128]{2,1,0:T(4,128)(2,1)} %bitcast.9), calls=%async_computation.3 | async-start | bytes 262144 | tf_op jit(solution)/shard_map/all_to_all | solution.py:381
  78.5 13.8 %collective-permute-start = (bf16[512,256]{1,0:T(8,128)(2,1)S(1)}, bf16[512,256]{1,0:T(8,128)(2,1)S(1)}, u32[]{:S(2)}, u32[]{:S(2)}) collective-permute-start(bf16[512,256]{1,0:T(8,128)(2,1)S(1)} %get-tuple-element.22), channel_id=1, source_target_pairs={{0,1},{1,2},{2,3},{3,0},{4,5},{5,6},{6,7},{7,4},{8,9},{9,10},{10,1... | collective-permute-start | bytes 786440 | tf_op jit(solution)/shard_map/ppermute | solution.py:376
  80.5 11.8 %collective-permute-start.2 = (bf16[512,256]{1,0:T(8,128)(2,1)S(1)}, bf16[512,256]{1,0:T(8,128)(2,1)S(1)}, u32[]{:S(2)}, u32[]{:S(2)}) collective-permute-start(bf16[512,256]{1,0:T(8,128)(2,1)S(1)} %get-tuple-element.26), channel_id=1, source_target_pairs={{0,3},{1,0},{2,1},{3,2},{4,7},{5,4},{6,5},{7,6},{8,11},{9,8},{10,9... | collective-permute-start | bytes 786440 | tf_op jit(solution)/shard_map/ppermute | solution.py:376

commit v5 on v4

--- a/solution.py
+++ b/solution.py
@@ -253,20 +253,27 @@
     out_ref[...] = value.astype(jnp.bfloat16)
 
 
-def ranked_kernel(arrived_ref, out_ref):
-    count = out_ref.shape[0]
-    line = iota((1, 2 * count), 1)
-    row = iota((count, 1), 0)
-    for half in range(2):
-        pick = jnp.where(line == 2 * row + half, 1.0, 0.0).astype(jnp.bfloat16)
-        out_ref[:, half * LANES:(half + 1) * LANES] = jnp.dot(
-            pick, arrived_ref[...], preferred_element_type=jnp.float32
-        ).astype(jnp.bfloat16)
+def ranked_kernel(arrived_ref, out_hbm, made_ref, sems):
+    count = made_ref.shape[0]
+    leaving = []
+    for block in range(2):
+        at = slice(block * count // 2, (block + 1) * count // 2)
+        line = iota((1, count), 1)
+        row = iota((count // 2, 1), 0)
+        for half in range(2):
+            pick = jnp.where(line == 2 * row + half, 1.0, 0.0).astype(jnp.bfloat16)
+            made_ref[at, half * LANES:(half + 1) * LANES] = jnp.dot(
+                pick, arrived_ref[block * count:(block + 1) * count], preferred_element_type=jnp.float32
+            ).astype(jnp.bfloat16)
+        leaving.append(pltpu.make_async_copy(made_ref.at[at], out_hbm.at[at], sems.at[block]))
+        leaving[block].start()
+    for copy in leaving:
+        copy.wait()
 
 
 def refresh_kernel(got_ref, *refs):
-    *term_refs, out_ref = refs
-    slots, width = out_ref.shape
+    *term_refs, out_hbm, made_ref, sems = refs
+    slots, width = made_ref.shape
     _, sources, _ = got_ref.shape
     cap = slots // sources
     meta = got_ref[2 * cap].astype(jnp.float32)
@@ -278,9 +285,17 @@
         parts.append(jnp.where(meta[:, k:k + 1] >= 0.0, own + mixed, 0.0).astype(jnp.bfloat16))
     updated = jnp.concatenate(parts, axis=0)
     line = iota((1, slots), 1)
-    row = iota((slots, 1), 0)
-    pick = jnp.where((line & (sources - 1)) * cap + line // sources == row, 1.0, 0.0).astype(jnp.bfloat16)
-    out_ref[...] = jnp.dot(pick, updated, preferred_element_type=jnp.float32).astype(jnp.bfloat16)
+    line = (line & (sources - 1)) * cap + line // sources
+    leaving = []
+    for half in range(2):
+        at = slice(half * slots // 2, (half + 1) * slots // 2)
+        row = iota((slots // 2, 1), 0) + half * slots // 2
+        pick = jnp.where(line == row, 1.0, 0.0).astype(jnp.bfloat16)
+        made_ref[at, :] = jnp.dot(pick, updated, preferred_element_type=jnp.float32).astype(jnp.bfloat16)
+        leaving.append(pltpu.make_async_copy(made_ref.at[at], out_hbm.at[at], sems.at[half]))
+        leaving[half].start()
+    for copy in leaving:
+        copy.wait()
 
 
 def call(kernel, out, args, scratch=(), smem=(), hbm=(), out_hbm=None, cost=None, vmem=VMEM):
@@ -387,12 +402,16 @@
         ranked_kernel,
         jax.ShapeDtypeStruct((owners * 2, width), bf16),
         (arrived.reshape(owners * 4, LANES),),
+        scratch=[pltpu.VMEM((owners * 2, width), bf16), pltpu.SemaphoreType.DMA((2,))],
+        out_hbm=(owners * 2, width),
         cost=pl.CostEstimate(flops=PICK_FLOPS, bytes_accessed=1 << 20, transcendentals=0),
     )
     refreshed = call(
         refresh_kernel,
         jax.ShapeDtypeStruct((slots, width), bf16),
         (got, *terms),
+        scratch=[pltpu.VMEM((slots, width), bf16), pltpu.SemaphoreType.DMA((2,))],
+        out_hbm=(slots, width),
         cost=pl.CostEstimate(flops=300_000_000, bytes_accessed=1 << 20, transcendentals=0),
     )
     return refreshed[None], ranked[None]

time: 94 us -> 93.9 us (level)
  no operation moved by 1% of the time
where the time goes in v5:
time: 93.9 us; the launch traced here: 93.4 us
  blocking collectives  53.6 us (57%)
  starting transfers between devices  22 us (23%)
  Pallas kernels  10.4 us (11%)
  waiting for transfers between devices  6.33 us (7%)
    all_to_all x1, blocking collectives, local(): lax.all_to_all(sent.reshape(owners, CHUNK // 2, 2, LANES), 'users', split...  35 us
    all_to_all x1, blocking collectives, local(): lax.all_to_all(jnp.broadcast_to(own, (groups,) + own.shape), 'heads', spl...  18.6 us
    ppermute x3, starting transfers between devices, passed(): lax.ppermute(term, 'heads', [(g, (g + shift) % groups) for g in range(gro...  11.3 us
    pallas_call x5, Pallas kernels, call(): pl.pallas_call(kernel, out_shape=out, in_specs=specs, out_specs=jax.tree....  10.4 us
    all_to_all x1, starting transfers between devices, local(): lax.all_to_all(outgoing.reshape(owners, 4, LANES), 'users', split_axis=0,...  7.36 us
    all_to_all x1, waiting for transfers between devices, local(): lax.all_to_all(outgoing.reshape(owners, 4, LANES), 'users', split_axis=0,...  6.32 us
    all_to_all x1, starting transfers between devices, local(): lax.all_to_all(edge, 'heads', split_axis=0, concat_axis=0, tiled=True)  3.28 us
  transfers between devices with their start and end apart: 5, of which 1 were waited for; matrix products, arithmetic and copies ran while one was open for 0% of the time, Pallas kernels for 2%

profile of v5, /device:TPU:1, one launch (start us, length us, event | category | flops | bytes accessed | tf_op | source)
XLA Modules:
  0.0 93.4 jit_solution(13610335677961766382)
XLA Ops:
  0.6 2.2 %shard_map.131 = bf16[1280,128]{1,0:T(8,128)(2,1)} custom-call(s32[1,256]{1,0:T(1,128)} %bitcast.22, s32[1,256]{1,0:T(1,128)} %bitcast.23, bf16[256,256]{1,0:T(8,128)(2,1)} %events_hbm.1, f32[1,1024]{1,0:T(1,128)} %bitcast.21, s32[1,2]{1,0:T(1,128)} %len_hbm.1, s32[1,2]{1,0:T(1,128)} %rank_hbm.1), custom_call_target="tpu_custom_call" | custom-call | tf_op jit(solution)/shard_map/pallas_call | solution.py:306
  2.8 35.0 %all_to_all.20 = bf16[128,5,2,128]{3,2,1,0:T(2,128)(2,1)S(1)} all-to-all(bf16[128,5,2,128]{3,2,1,0:T(2,128)(2,1)} %bitcast.19), channel_id=1, replica_groups=mesh['users'=128,'heads'=4] {'users'}, dimensions={0} | all-to-all | bytes 655360 | tf_op jit(solution)/shard_map/all_to_all | solution.py:351
  37.9 0.0 copy-start.4
  37.9 0.0 copy-start.5
  38.0 0.2 broadcast_in_dim.9
  38.2 0.0 copy-start
  38.2 0.0 copy-start.1
  38.2 0.0 copy-start.2
  38.2 0.0 copy-start.3
  38.2 18.6 %all_to_all.21.rows_ref = bf16[4,8,128,128]{3,2,1,0:T(8,128)(2,1)S(1)} all-to-all(bf16[4,8,128,128]{3,2,1,0:T(8,128)(2,1)S(1)} %broadcast_in_dim.9), channel_id=1, replica_groups=mesh['users'=128,'heads'=4] {'heads'}, dimensions={0} | all-to-all | bytes 2097152 | tf_op jit(solution)/shard_map/all_to_all | solution.py:356
  56.8 0.0 copy-done.4
  56.8 0.0 copy-done.5
  56.8 0.0 copy-done
  56.8 0.0 copy-done.1
  56.8 0.0 copy-done.2
  56.8 0.0 copy-done.3
  56.8 5.2 %shard_map.132 = (bf16[512,256]{1,0:T(8,128)(2,1)S(1)}, bf16[512,256]{1,0:T(8,128)(2,1)S(1)}, bf16[512,256]{1,0:T(8,128)(2,1)S(1)}, bf16[512,256]{1,0:T(8,128)(2...) custom-call(bf16[4,8,128,128]{3,2,1,0:T(8,128)(2,1)S(1)} %all_to_all.21.rows_ref, ...), custom_call_target="tpu_custom_call" | custom-call | tf_op jit(solution)/shard_map/pallas_call | solution.py:306
  62.0 3.3 %all-to-all-start.2 = ((bf16[4,16,256]{2,1,0:T(8,128)(2,1)}), bf16[4,16,256]{2,1,0:T(8,128)(2,1)S(1)}, u32[]{:S(2)}, u32[]{:S(2)}) async-start(bf16[4,16,256]{2,1,0:T(8,128)(2,1)} %get-tuple-element.19), calls=%async_computation.2 | async-start | bytes 65536 | tf_op jit(solution)/shard_map/all_to_all | solution.py:383
  65.3 4.8 %collective-permute-start.1 = (bf16[512,256]{1,0:T(8,128)(2,1)S(1)}, bf16[512,256]{1,0:T(8,128)(2,1)S(1)}, u32[]{:S(2)}, u32[]{:S(2)}) collective-permute-start(bf16[512,256]{1,0:T(8,128)(2,1)S(1)} %get-tuple-element.24), channel_id=1, source_target_pairs={{0,2},{1,3},{2,0},{3,1},{4,6},{5,7},{6,4},{7,5},{8,10},{9,11},{10,... | collective-permute-start | bytes 786440 | tf_op jit(solution)/shard_map/ppermute | solution.py:391
  70.2 0.0 all-to-all-done.2.terms_ref
  70.2 1.0 %shard_map.133 = bf16[512,128]{1,0:T(8,128)(2,1)} custom-call(f32[24,256]{1,0:T(8,128)S(1)} %get-tuple-element.18.base_ref, bf16[4,16,256]{2,1,0:T(8,128)(2,1)S(1)} %all-to-all-done.2.terms_ref), custom_call_target="tpu_custom_call" | custom-call | flops 30000001024 | bytes 1048576 | tf_op jit(solution)/shard_map/pallas_call | solution.py:306
  71.2 7.4 %all-to-all-start.3 = ((bf16[128,4,128]{2,1,0:T(4,128)(2,1)}), bf16[128,4,128]{2,1,0:T(4,128)(2,1)S(1)}, u32[]{:S(2)}, u32[]{:S(2)}) async-start(bf16[128,4,128]{2,1,0:T(4,128)(2,1)} %bitcast.9), calls=%async_computation.3 | async-start | bytes 262144 | tf_op jit(solution)/shard_map/all_to_all | solution.py:396
  78.5 2.0 %collective-permute-start = (bf16[512,256]{1,0:T(8,128)(2,1)S(1)}, bf16[512,256]{1,0:T(8,128)(2,1)S(1)}, u32[]{:S(2)}, u32[]{:S(2)}) collective-permute-start(bf16[512,256]{1,0:T(8,128)(2,1)S(1)} %get-tuple-element.22), channel_id=1, source_target_pairs={{0,1},{1,2},{2,3},{3,0},{4,5},{5,6},{6,7},{7,4},{8,9},{9,10},{10,1... | collective-permute-start | bytes 786440 | tf_op jit(solution)/shard_map/ppermute | solution.py:391
  80.5 4.5 %collective-permute-start.2 = (bf16[512,256]{1,0:T(8,128)(2,1)S(1)}, bf16[512,256]{1,0:T(8,128)(2,1)S(1)}, u32[]{:S(2)}, u32[]{:S(2)}) collective-permute-start(bf16[512,256]{1,0:T(8,128)(2,1)S(1)} %get-tuple-element.26), channel_id=1, source_target_pairs={{0,3},{1,0},{2,1},{3,2},{4,7},{5,4},{6,5},{7,6},{8,11},{9,8},{10,9... | collective-permute-start | bytes 786440 | tf_op jit(solution)/shard_map/ppermute | solution.py:391
  85.1 0.0 collective-permute-done.1.refs_2_
  85.1 6.3 %all-to-all-done.3 = bf16[128,4,128]{2,1,0:T(4,128)(2,1)S(1)} async-done(((bf16[128,4,128]{2,1,0:T(4,128)(2,1)}), bf16[128,4,128]{2,1,0:T(4,128)(2,1)S(1)}, u32[]{:S(2)}, u32[]{:S(2)}) %all-to-all-start.3) | async-done | bytes 131104 | tf_op jit(solution)/shard_map/all_to_all | solution.py:396
  91.4 0.9 shard_map.135
  92.3 0.0 collective-permute-done.refs_1_
  92.3 0.0 collective-permute-done.2.refs_3_
  92.3 1.1 %shard_map.134 = bf16[512,256]{1,0:T(8,128)(2,1)} custom-call(bf16[10,128,128]{2,1,0:T(8,128)(2,1)S(1)} %bitcast.15, bf16[512,256]{1,0:T(8,128)(2,1)S(1)} %get-tuple-element.17.refs_0_, bf16[512,256]{1,0:T(8,128)(2,1)S(1)} %collective-permute-done.refs_1_, bf16[512,256]{1,0:T(8,128)(2,1)S(1)} %collective-permute-done.1.refs_2_, ...), custom_call_target="tpu_custom_call" | custom-call | flops 300000000 | bytes 1048576 | tf_op jit(solution)/shard_map/pallas_call | solution.py:306
  (2 shorter events, 0.1 us)
Async XLA Ops:
  37.9 18.9 %copy-start.4 = (bf16[1,2,512,256]{3,2,1,0:T(8,128)(2,1)S(1)}, bf16[1,2,512,256]{3,2,1,0:T(8,128)(2,1)}, u32[]{:S(2)}) copy-start(bf16[1,2,512,256]{3,2,1,0:T(8,128)(2,1)} %param.16) | copy-start | bytes 1572868
  37.9 18.9 %copy-start.5 = (bf16[256,1024]{1,0:T(8,128)(2,1)S(1)}, bf16[256,1024]{1,0:T(8,128)(2,1)}, u32[]{:S(2)}) copy-start(bf16[256,1024]{1,0:T(8,128)(2,1)} %wo_ref.1) | copy-start | bytes 1572868
  38.2 18.6 %copy-start = (bf16[1024,256]{1,0:T(8,128)(2,1)S(1)}, bf16[1024,256]{1,0:T(8,128)(2,1)}, u32[]{:S(2)}) copy-start(bf16[1024,256]{1,0:T(8,128)(2,1)} %wq_ref.1) | copy-start | bytes 1572868
  38.2 18.6 %copy-start.1 = (bf16[1024,256]{1,0:T(8,128)(2,1)S(1)}, bf16[1024,256]{1,0:T(8,128)(2,1)}, u32[]{:S(2)}) copy-start(bf16[1024,256]{1,0:T(8,128)(2,1)} %wk_ref.1) | copy-start | bytes 1572868
  38.2 18.6 %copy-start.2 = (bf16[1024,256]{1,0:T(8,128)(2,1)S(1)}, bf16[1024,256]{1,0:T(8,128)(2,1)}, u32[]{:S(2)}) copy-start(bf16[1024,256]{1,0:T(8,128)(2,1)} %wv_ref.1) | copy-start | bytes 1572868
  38.2 18.6 %copy-start.3 = (bf16[1,2,512,256]{3,2,1,0:T(8,128)(2,1)S(1)}, bf16[1,2,512,256]{3,2,1,0:T(8,128)(2,1)}, u32[]{:S(2)}) copy-start(bf16[1,2,512,256]{3,2,1,0:T(8,128)(2,1)} %param.15) | copy-start | bytes 1572868
  62.0 8.1 %all-to-all-start.2 = ((bf16[4,16,256]{2,1,0:T(8,128)(2,1)}), bf16[4,16,256]{2,1,0:T(8,128)(2,1)S(1)}, u32[]{:S(2)}, u32[]{:S(2)}) async-start(bf16[4,16,256]{2,1,0:T(8,128)(2,1)} %get-tuple-element.19), calls=%async_computation.2 | async-start | bytes 65536 | tf_op jit(solution)/shard_map/all_to_all | solution.py:383
  65.3 19.7 %collective-permute-start.1 = (bf16[512,256]{1,0:T(8,128)(2,1)S(1)}, bf16[512,256]{1,0:T(8,128)(2,1)S(1)}, u32[]{:S(2)}, u32[]{:S(2)}) collective-permute-start(bf16[512,256]{1,0:T(8,128)(2,1)S(1)} %get-tuple-element.24), channel_id=1, source_target_pairs={{0,2},{1,3},{2,0},{3,1},{4,6},{5,7},{6,4},{7,5},{8,10},{9,11},{10,... | collective-permute-start | bytes 786440 | tf_op jit(solution)/shard_map/ppermute | solution.py:391
  71.2 20.2 %all-to-all-start.3 = ((bf16[128,4,128]{2,1,0:T(4,128)(2,1)}), bf16[128,4,128]{2,1,0:T(4,128)(2,1)S(1)}, u32[]{:S(2)}, u32[]{:S(2)}) async-start(bf16[128,4,128]{2,1,0:T(4,128)(2,1)} %bitcast.9), calls=%async_computation.3 | async-start | bytes 262144 | tf_op jit(solution)/shard_map/all_to_all | solution.py:396
  78.5 13.7 %collective-permute-start = (bf16[512,256]{1,0:T(8,128)(2,1)S(1)}, bf16[512,256]{1,0:T(8,128)(2,1)S(1)}, u32[]{:S(2)}, u32[]{:S(2)}) collective-permute-start(bf16[512,256]{1,0:T(8,128)(2,1)S(1)} %get-tuple-element.22), channel_id=1, source_target_pairs={{0,1},{1,2},{2,3},{3,0},{4,5},{5,6},{6,7},{7,4},{8,9},{9,10},{10,1... | collective-permute-start | bytes 786440 | tf_op jit(solution)/shard_map/ppermute | solution.py:391
  80.5 11.7 %collective-permute-start.2 = (bf16[512,256]{1,0:T(8,128)(2,1)S(1)}, bf16[512,256]{1,0:T(8,128)(2,1)S(1)}, u32[]{:S(2)}, u32[]{:S(2)}) collective-permute-start(bf16[512,256]{1,0:T(8,128)(2,1)S(1)} %get-tuple-element.26), channel_id=1, source_target_pairs={{0,3},{1,0},{2,1},{3,2},{4,7},{5,4},{6,5},{7,6},{8,11},{9,8},{10,9... | collective-permute-start | bytes 786440 | tf_op jit(solution)/shard_map/ppermute | solution.py:391
